TPU v7x, 256 devices: a whole 4x4x8 slice. The times are simulated.
256 devices in a mesh: grp: 16 (over z, core), cp: 16 (over y, x).
Axes of the slice: x: 4, y: 4, z: 8, core: 2. Of those that a mesh axis runs over, the one named last changes fastest.
Arguments:
- clean_hidden: bfloat16 [16, 2048, 5120], P('grp', 'cp'), may hold values from -6 to 6
- noisy_hidden: bfloat16 [16, 2048, 5120], P('grp', 'cp'), may hold values from -6 to 6
- noisy_query: bfloat16 [16, 2048, 1024], P('grp', 'cp'), may hold values from -288 to 288
- out_grad: bfloat16 [16, 2048, 1024], P('grp', 'cp'), may hold values from -6 to 6
- kv_weight: bfloat16 [5120, 256], replicated, may hold values from -0.078125 to 0.078125
- key_gain: float32 [128], replicated, may hold values from 0.5 to 2
- doc_lengths: int32 [16, 4], P('grp'), may hold values from 1 to 26, 32 in all within a row
- clean_place: int32 [16, 32], P('grp'), may hold values from 0 to 31, each once within a row
- noisy_place: int32 [16, 32], P('grp'), may hold values from 0 to 31, each once within a row
Outputs:
- attention_out: bfloat16 [16, 2048, 1024], P('grp', 'cp')
- query_grad: bfloat16 [16, 2048, 1024], P('grp', 'cp')
- kv_weight_grad: bfloat16 [5120, 256], P(('grp', 'cp'))
Inputs may be any that keep to these rules, and one draw needn't show every extreme that they name: `doc_lengths`: each group's 4 lengths sum to 32; in every group the longest is exactly 32 - 3 * max(1, 2). `clean_place`: each group's row is a permutation of the slots. `noisy_place`: each group's row is a permutation of the slots.
All inputs are finite; a program needn't handle non-finite values.
Results may differ from a plain program's by a relative error of at most 0.033.
The roundings to bfloat16 on the way count: a program that leaves them out, or rounds other values in their place, can miss the bound.
Values may be sent and summed in bfloat16 or wider, within the bound.
No kernel may reach another device: no remote copies, remote signals or barrier semaphores. Data moves between devices by JAX's collectives and lax.ppermute only.
A program may use at most 128 MiB of HBM per device.

v0:
```python
import jax
import jax.numpy as jnp
from jax import lax
from jax.sharding import PartitionSpec as P

BLK = 64


EPSILON = 1e-06
NEGATIVE = -1e30


def project_rows(hidden_rows, kv_weight, key_gain):
    head_size = key_gain.shape[0]
    joined = jnp.dot(hidden_rows, kv_weight, preferred_element_type=jnp.float32)
    pre_key = joined[:, :head_size]
    inverse = lax.rsqrt(jnp.mean(pre_key * pre_key, axis=1, keepdims=True) + EPSILON)
    key_rows = (pre_key * inverse * key_gain).astype(jnp.bfloat16)
    value_rows = joined[:, head_size:].astype(jnp.bfloat16)
    return (jnp.concatenate([key_rows, value_rows], axis=1), pre_key, inverse)


def norm_back(key_grads, pre_key, inverse, key_gain):
    scaled = key_grads * key_gain
    inner_sum = jnp.mean(scaled * pre_key, axis=1, keepdims=True)
    return inverse * scaled - pre_key * inverse * inverse * inverse * inner_sum


def lookup(lookup_table, wanted):
    matches = wanted[:, None] == jnp.arange(lookup_table.shape[0], dtype=jnp.int32)[None, :]
    return jnp.sum(jnp.where(matches, lookup_table[None, :], 0), axis=1)


def invert(placement):
    slot_ids = jnp.arange(placement.shape[0], dtype=jnp.int32)
    matches = placement[None, :] == slot_ids[:, None]
    return jnp.sum(jnp.where(matches, slot_ids[None, :], 0), axis=1)


def row_tables(order_table, doc_of, begin_row, amount):
    slot_ids = (begin_row + jnp.arange(amount, dtype=jnp.int32)) // BLK
    logical = lookup(order_table, slot_ids)
    return (logical, lookup(doc_of, logical))


def visible(query_log, query_doc, key_log, key_doc):
    return (key_doc[None, :] == query_doc[:, None]) & (key_log[None, :] < query_log[:, None])


def scores(queries, key_rows, allowed):
    scaling = queries.shape[-1] ** (-0.5)
    raw_scores = (
        jnp.einsum("rhd,kd->hrk", queries, key_rows, preferred_element_type=jnp.float32) * scaling
    )
    return jnp.where(allowed[None], raw_scores, NEGATIVE)


def stats_add(state, queries, key_rows, allowed):
    row_max, sum_exp = state
    current = scores(queries, key_rows, allowed)
    new_max = jnp.maximum(row_max, jnp.max(current, axis=2))
    sum_exp = sum_exp * jnp.exp(row_max - new_max) + jnp.sum(
        jnp.exp(current - new_max[:, :, None]), axis=2
    )
    return (new_max, sum_exp)


def output_add(accumulated, queries, kv_rows, allowed, log_total):
    head_size = queries.shape[-1]
    attn_prob = jnp.exp(
        scores(queries, kv_rows[:, :head_size], allowed) - log_total[:, :, None]
    ).astype(jnp.bfloat16)
    return accumulated + jnp.einsum(
        "hrk,kd->rhd", attn_prob, kv_rows[:, head_size:], preferred_element_type=jnp.float32
    )


def back_core(queries, grad_rows, kv_rows, allowed, log_total, row_delta):
    head_size = queries.shape[-1]
    attn_prob = jnp.exp(scores(queries, kv_rows[:, :head_size], allowed) - log_total[:, :, None])
    grad_prob = jnp.einsum(
        "rhd,kd->hrk", grad_rows, kv_rows[:, head_size:], preferred_element_type=jnp.float32
    )
    score_grad = (attn_prob * (grad_prob - row_delta[:, :, None])).astype(jnp.bfloat16)
    return (score_grad, attn_prob.astype(jnp.bfloat16))


def grad_of_query(score_grad, key_rows):
    return jnp.einsum(
        "hrk,kd->rhd", score_grad, key_rows, preferred_element_type=jnp.float32
    ) * key_rows.shape[-1] ** (-0.5)


def grad_of_keys(score_grad, prob_low, queries, grad_rows):
    scaling = queries.shape[-1] ** (-0.5)
    key_grads = (
        jnp.einsum("hrk,rhd->kd", score_grad, queries, preferred_element_type=jnp.float32) * scaling
    )
    value_grads = jnp.einsum("hrk,rhd->kd", prob_low, grad_rows, preferred_element_type=jnp.float32)
    return jnp.concatenate([key_grads, value_grads], axis=1)


def per_device(
    clean_hidden,
    noisy_hidden,
    noisy_query,
    out_grad,
    kv_weight,
    key_gain,
    doc_lengths,
    clean_place,
    noisy_place,
):
    cp_index = lax.axis_index("cp")
    tok_rows = clean_hidden.shape[1]
    head_size = key_gain.shape[0]
    clean_rows = clean_hidden[0]
    noisy_rows = noisy_hidden[0]
    clean_kv, clean_pre, clean_inv = project_rows(clean_rows, kv_weight, key_gain)
    noisy_kv, noisy_pre, noisy_inv = project_rows(noisy_rows, kv_weight, key_gain)
    queries = noisy_query[0].reshape(tok_rows, -1, head_size)
    grad_rows = out_grad[0].reshape(tok_rows, -1, head_size)
    head_count = queries.shape[1]
    clean_order = invert(clean_place[0])
    noisy_order = invert(noisy_place[0])
    block_ids = jnp.arange(clean_place.shape[1], dtype=jnp.int32)
    doc_ends = jnp.cumsum(doc_lengths[0])
    doc_of = jnp.sum((doc_ends[None, :] <= block_ids[:, None]).astype(jnp.int32), axis=1)
    first_row = cp_index * tok_rows
    query_log, query_doc = row_tables(noisy_order, doc_of, first_row, tok_rows)
    clean_log, clean_doc = row_tables(clean_order, doc_of, first_row, tok_rows)
    local_block = jnp.arange(tok_rows, dtype=jnp.int32) // BLK
    self_allowed = local_block[:, None] == local_block[None, :]

    def clean_allowed(begin_row, amount):
        key_log, key_doc = row_tables(clean_order, doc_of, begin_row, amount)
        return visible(query_log, query_doc, key_log, key_doc)

    self_scores = scores(queries, noisy_kv[:, :head_size], self_allowed)
    self_max = jnp.max(self_scores, axis=2)
    initial = (self_max, jnp.sum(jnp.exp(self_scores - self_max[:, :, None]), axis=2))
    shard_rows = lax.all_gather(clean_kv[:, :head_size], "cp", axis=0, tiled=True)
    row_max, sum_exp = stats_add(
        initial, queries, shard_rows, clean_allowed(jnp.int32(0), shard_rows.shape[0])
    )
    log_total = row_max + jnp.log(sum_exp)
    start_out = output_add(
        jnp.zeros((tok_rows, head_count, head_size), jnp.float32),
        queries,
        noisy_kv,
        self_allowed,
        log_total,
    )
    shard_rows = lax.all_gather(clean_kv, "cp", axis=0, tiled=True)
    summed_out = output_add(
        start_out, queries, shard_rows, clean_allowed(jnp.int32(0), shard_rows.shape[0]), log_total
    )
    attention = summed_out.astype(jnp.bfloat16)
    row_delta = jnp.sum(grad_rows.astype(jnp.float32) * attention.astype(jnp.float32), axis=2).T
    self_grad, self_prob = back_core(
        queries, grad_rows, noisy_kv, self_allowed, log_total, row_delta
    )
    start_query = grad_of_query(self_grad, noisy_kv[:, :head_size])
    noisy_kv_grad = grad_of_keys(self_grad, self_prob, queries, grad_rows)
    start_buffer = jnp.zeros((1, 1), jnp.float32)
    shard_rows = lax.all_gather(clean_kv, "cp", axis=0, tiled=True)
    query_sum = start_query
    buffer = start_buffer
    amount = shard_rows.shape[0]
    score_grad, prob_low = back_core(
        queries, grad_rows, shard_rows, clean_allowed(jnp.int32(0), amount), log_total, row_delta
    )
    query_sum = query_sum + grad_of_query(score_grad, shard_rows[:, :head_size])
    query_sum, buffer = (query_sum, buffer)
    every_max, every_delta = (
        lax.all_gather(log_total.T, "cp", axis=0, tiled=True),
        lax.all_gather(row_delta.T, "cp", axis=0, tiled=True),
    )
    query_part = lax.all_gather(noisy_query[0], "cp", axis=0, tiled=True)
    grad_part = lax.all_gather(out_grad[0], "cp", axis=0, tiled=True)
    amount = query_part.shape[0]
    query_block = query_part.reshape(amount, head_count, head_size)
    grad_block = grad_part.reshape(amount, head_count, head_size)
    part_log, part_doc = row_tables(noisy_order, doc_of, jnp.int32(0), amount)
    allowed = visible(part_log, part_doc, clean_log, clean_doc)
    part_max = every_max.T
    part_delta = every_delta.T
    score_grad, prob_low = back_core(
        query_block, grad_block, clean_kv, allowed, part_max, part_delta
    )
    clean_kv_grad = grad_of_keys(score_grad, prob_low, query_block, grad_block)
    clean_row_grad = jnp.concatenate(
        [
            norm_back(clean_kv_grad[:, :head_size], clean_pre, clean_inv, key_gain),
            clean_kv_grad[:, head_size:],
        ],
        axis=1,
    ).astype(jnp.bfloat16)
    noisy_row_grad = jnp.concatenate(
        [
            norm_back(noisy_kv_grad[:, :head_size], noisy_pre, noisy_inv, key_gain),
            noisy_kv_grad[:, head_size:],
        ],
        axis=1,
    ).astype(jnp.bfloat16)
    stacked_rows = jnp.concatenate([clean_rows, noisy_rows], axis=0)
    stacked_grad = jnp.concatenate([clean_row_grad, noisy_row_grad], axis=0)
    weight_share = lax.psum_scatter(
        lax.dot_general(
            stacked_rows, stacked_grad, (((0,), (0,)), ((), ())), preferred_element_type=jnp.float32
        ),
        ("grp", "cp"),
        scatter_dimension=0,
        tiled=True,
    )
    return (
        attention.reshape(1, tok_rows, head_count * head_size),
        query_sum.astype(jnp.bfloat16).reshape(1, tok_rows, head_count * head_size),
        weight_share.astype(jnp.bfloat16),
    )


def solution(mesh):
    in_specs = (
        P("grp", "cp", None),
        P("grp", "cp", None),
        P("grp", "cp", None),
        P("grp", "cp", None),
        P(),
        P(),
        P("grp", None),
        P("grp", None),
        P("grp", None),
    )
    out_specs = (P("grp", "cp", None), P("grp", "cp", None), P(("grp", "cp"), None))
    return jax.shard_map(
        per_device, mesh=mesh, in_specs=in_specs, out_specs=out_specs, check_vma=False
    )
```

profile of v0, /device:TPU:2, one launch (start us, length us, event | category | flops | bytes accessed | tf_op | source)
XLA Modules:
  0.0 1152.0 jit_solution(2145173054112520866)
XLA Ops:
  8.9 1.8 fusion.75
  12.4 1.8 copy.169
  14.2 1.8 copy.119
  18.0 1.8 fusion.77
  19.9 24.1 %all_gather.19 = bf16[2048,128]{1,0:T(8,128)(2,1)S(1)} all-gather(bf16[128,128]{1,0:T(8,128)(2,1)S(1)} %multiply_convert_fusion), channel_id=1, replica_groups=mesh['grp'=16,'cp'=16] {'cp'}, dimensions={0}, use_global_device_ids=true | all-gather | bytes 557056 | tf_op jit(solution)/shard_map/all_gather | solution.py:142
  47.1 2.4 fusion.9
  51.4 23.0 %all_gather.22 = f32[2048,8]{0,1:T(8,128)} all-gather(f32[128,8]{0,1:T(8,128)S(1)} %fusion.70), channel_id=1, replica_groups=mesh['grp'=16,'cp'=16] {'cp'}, dimensions={0}, use_global_device_ids=true | all-gather | bytes 69632 | tf_op jit(solution)/shard_map/all_gather | solution.py:176
  76.7 2.4 fusion.48
  79.1 3.2 copy-done.1
  82.4 2.1 fusion.17
  85.5 24.9 %all_gather.24 = f32[2048,8]{0,1:T(8,128)} all-gather(f32[128,8]{0,1:T(8,128)S(1)} %get-tuple-element.72), channel_id=1, replica_groups=mesh['grp'=16,'cp'=16] {'cp'}, dimensions={0}, use_global_device_ids=true | all-gather | bytes 69632 | tf_op jit(solution)/shard_map/all_gather | solution.py:177
  112.1 15.7 %all-gather.8.cloned.1.call-done = bf16[1,2048,1024]{1,2,0:T(8,128)(2,1)} async-done(((bf16[1,128,1024]{1,2,0:T(8,128)(2,1)}), bf16[1,2048,1024]{1,2,0:T(8,128)(2,1)}) %all-gather.8.cloned.1.call-update) | async-done | bytes 4194320 | tf_op jit(solution)/shard_map/all_gather | solution.py:179
  127.8 6.7 fusion.62
  134.5 58.5 %all-gather.10.cloned.1.call-done = bf16[1,2048,1024]{1,2,0:T(8,128)(2,1)} async-done(((bf16[1,128,1024]{1,2,0:T(8,128)(2,1)}), bf16[1,2048,1024]{1,2,0:T(8,128)(2,1)}) %all-gather.10.cloned.1.call-update) | async-done | bytes 4194320 | tf_op jit(solution)/shard_map/all_gather | solution.py:180
  193.0 7.4 fusion.42
  200.4 9.9 multiply_reduce_fusion.2
  211.9 5.0 fusion.21
  217.0 681.1 %fusion = f32[24,256]{1,0:T(8,128)} fusion(f32[5120,256]{1,0:T(8,128)} %fusion.21), kind=kCustom, calls=%all-reduce-scatter | all-reduce-scatter fusion | flops 1572865 | bytes 5267456
  899.4 1.9 collective-permute-start.41
  901.3 1.9 collective-permute-start.40
  903.9 6.3 collective-permute-start.42
  910.2 1.9 collective-permute-start.39
  912.0 1.9 collective-permute-start.38
  913.9 1.9 collective-permute-start.37
  915.8 1.9 collective-permute-start.36
  917.7 1.9 collective-permute-start.35
  919.5 1.9 collective-permute-start.34
  921.4 1.9 collective-permute-start.33
  923.3 11.8 %collective-permute-start.32 = (bf16[24,256]{1,0:T(8,128)(2,1)}, bf16[24,256]{1,0:T(8,128)(2,1)}, u32[]{:S(2)}, u32[]{:S(2)}) collective-permute-start(bf16[24,256]{1,0:T(8,128)(2,1)} %convert.118), channel_id=1, source_target_pairs={{0,33},{1,34},{2,35},{3,36},{4,37},{5,38},{6,39},{7,40},{8,41},{9,... | collective-permute-start | bytes 36872
  935.2 3.3 collective-permute-start.31
  938.5 2.2 collective-permute-start.30
  940.7 5.6 collective-permute-start.29
  946.3 1.9 collective-permute-start.28
  948.2 1.9 collective-permute-start.27
  950.1 1.9 collective-permute-start.26
  952.0 1.9 collective-permute-start.25
  953.9 3.7 collective-permute-start.24
  957.6 2.6 collective-permute-start.23
  960.1 2.1 collective-permute-start.22
  962.2 1.9 collective-permute-start.21
  964.1 3.3 collective-permute-start.20
  967.4 1.9 collective-permute-start.19
  969.3 1.9 collective-permute-start.18
  971.2 3.8 collective-permute-start.17
  975.0 2.0 collective-permute-start.16
  977.0 2.0 collective-permute-start.15
  978.9 2.1 collective-permute-start.14
  981.0 5.5 collective-permute-start.13
  986.5 2.0 collective-permute-start.12
  988.5 1.9 collective-permute-start.11
  990.3 2.0 collective-permute-start.10
  992.3 3.8 collective-permute-start.9
  996.1 3.5 collective-permute-start.8
  999.5 5.7 collective-permute-start.7
  1005.2 13.1 %collective-permute-start.6 = (bf16[24,256]{1,0:T(8,128)(2,1)}, bf16[24,256]{1,0:T(8,128)(2,1)}, u32[]{:S(2)}, u32[]{:S(2)}) collective-permute-start(bf16[24,256]{1,0:T(8,128)(2,1)} %convert.118), channel_id=1, source_target_pairs={{0,7},{1,8},{2,9},{3,10},{4,11},{5,12},{6,13},{7,14},{8,15},{9,16}... | collective-permute-start | bytes 36872
  1018.4 13.1 %collective-permute-start.5 = (bf16[24,256]{1,0:T(8,128)(2,1)}, bf16[24,256]{1,0:T(8,128)(2,1)}, u32[]{:S(2)}, u32[]{:S(2)}) collective-permute-start(bf16[24,256]{1,0:T(8,128)(2,1)} %convert.118), channel_id=1, source_target_pairs={{0,6},{1,7},{2,8},{3,9},{4,10},{5,11},{6,12},{7,13},{8,14},{9,15},... | collective-permute-start | bytes 36872
  1031.5 7.6 fusion.25
  1039.1 12.8 %collective-permute-start.4 = (bf16[24,256]{1,0:T(8,128)(2,1)}, bf16[24,256]{1,0:T(8,128)(2,1)S(1)}, u32[]{:S(2)}, u32[]{:S(2)}) collective-permute-start(bf16[24,256]{1,0:T(8,128)(2,1)} %convert.118), channel_id=1, source_target_pairs={{0,5},{1,6},{2,7},{3,8},{4,9},{5,10},{6,11},{7,12},{8,13},{9,14},{... | collective-permute-start | bytes 36872
  1051.9 13.1 %collective-permute-start.3 = (bf16[24,256]{1,0:T(8,128)(2,1)}, bf16[24,256]{1,0:T(8,128)(2,1)S(1)}, u32[]{:S(2)}, u32[]{:S(2)}) collective-permute-start(bf16[24,256]{1,0:T(8,128)(2,1)} %convert.118), channel_id=1, source_target_pairs={{0,4},{1,5},{2,6},{3,7},{4,8},{5,9},{6,10},{7,11},{8,12},{9,13},{1... | collective-permute-start | bytes 36872
  1065.1 13.1 %collective-permute-start.2 = (bf16[24,256]{1,0:T(8,128)(2,1)}, bf16[24,256]{1,0:T(8,128)(2,1)S(1)}, u32[]{:S(2)}, u32[]{:S(2)}) collective-permute-start(bf16[24,256]{1,0:T(8,128)(2,1)} %convert.118), channel_id=1, source_target_pairs={{0,3},{1,4},{2,5},{3,6},{4,7},{5,8},{6,9},{7,10},{8,11},{9,12},{10... | collective-permute-start | bytes 36872
  1078.2 13.1 %collective-permute-start.1 = (bf16[24,256]{1,0:T(8,128)(2,1)}, bf16[24,256]{1,0:T(8,128)(2,1)S(1)}, u32[]{:S(2)}, u32[]{:S(2)}) collective-permute-start(bf16[24,256]{1,0:T(8,128)(2,1)} %convert.118), channel_id=1, source_target_pairs={{0,2},{1,3},{2,4},{3,5},{4,6},{5,7},{6,8},{7,9},{8,10},{9,11},{10,... | collective-permute-start | bytes 36872
  1091.3 13.1 %collective-permute-start = (bf16[24,256]{1,0:T(8,128)(2,1)}, bf16[24,256]{1,0:T(8,128)(2,1)}, u32[]{:S(2)}, u32[]{:S(2)}) collective-permute-start(bf16[24,256]{1,0:T(8,128)(2,1)} %convert.118), channel_id=1, source_target_pairs={{0,1},{1,2},{2,3},{3,4},{4,5},{5,6},{6,7},{7,8},{8,9},{9,10},{10,1... | collective-permute-start | bytes 36872
  1105.9 1.8 copy.139
  1109.7 35.1 %concatenate.22 = bf16[1044,256]{1,0:T(8,128)(2,1)S(1)} concatenate(bf16[12,256]{1,0:T(8,128)(2,1)} %collective-permute-done.42, bf16[24,256]{1,0:T(8,128)(2,1)} %collective-permute-done.41, bf16[24,256]{1,0:T(8,128)(2,1)} %collective-permute-done.40, bf16[24,256]{1,0:T(8,128)(2,1)} %collective-permute-done.39, bf16[24,256]{1,0:T(8,128)(2,1)} %collective-permute-done.38, ...), dimensions={0} | concatenate | bytes 1081344
  (143 shorter events, 23.1 us)
Async XLA Ops:
  7.2 37.3 %copy-start.21 = (f32[128]{0:T(128)S(1)}, f32[128]{0:T(128)}, u32[]{:S(2)}) copy-start(f32[128]{0:T(128)} %param.14) | copy-start | bytes 1540
  7.2 69.5 %all-gather.6.cloned.1.call-start = ((), (), s32[]{:S(2)}) async-start(), calls=%async_computation | async-start | bytes 1114112 | tf_op jit(solution)/shard_map/all_gather | solution.py:154
  10.7 36.3 %copy-start.11 = (f32[128,256]{1,0:T(8,128)}, f32[128,256]{1,0:T(8,128)S(1)}, u32[]{:S(2)}) copy-start(f32[128,256]{1,0:T(8,128)S(1)} %fusion.75) | copy-start | bytes 393220
  10.9 36.2 %copy-start.23 = (f32[128]{0:T(128)}, f32[128]{0:T(128)S(1)}, u32[]{:S(2)}) copy-start(f32[128]{0:T(128)S(1)} %add_rsqrt_fusion) | copy-start | bytes 1540
  11.6 35.4 %copy-start.13 = (bf16[128,128]{1,0:T(8,128)(2,1)}, bf16[128,128]{1,0:T(8,128)(2,1)S(1)}, u32[]{:S(2)}) copy-start(bf16[128,128]{1,0:T(8,128)(2,1)S(1)} %multiply_convert_fusion) | copy-start | bytes 98308
  12.3 115.5 %all-gather.8.cloned.1.call-start = ((), (), s32[]{:S(2)}) async-start(), calls=%async_computation.1 | async-start | bytes 4456448 | tf_op jit(solution)/shard_map/all_gather | solution.py:179
  14.2 178.8 %all-gather.10.cloned.1.call-start = ((), (), s32[]{:S(2)}) async-start(), calls=%async_computation.2 | async-start | bytes 4456448 | tf_op jit(solution)/shard_map/all_gather | solution.py:180
  44.4 67.0 %copy-start.22 = (f32[128]{0:T(128)}, f32[128]{0:T(128)S(1)}, u32[]{:S(2)}) copy-start(f32[128]{0:T(128)S(1)} %add_rsqrt_fusion.1) | copy-start | bytes 1540
  47.1 27.8 %copy-start.3 = (bf16[1,128,1024]{1,2,0:T(8,128)(2,1)S(1)}, bf16[1,128,1024]{1,2,0:T(8,128)(2,1)}, u32[]{:S(2)}) copy-start(bf16[1,128,1024]{1,2,0:T(8,128)(2,1)} %copy.119) | copy-start | bytes 786436
  49.5 27.2 %copy-start.2 = (bf16[1,128,1024]{1,2,0:T(8,128)(2,1)S(1)}, bf16[1,128,1024]{1,2,0:T(8,128)(2,1)}, u32[]{:S(2)}) copy-start(bf16[1,128,1024]{1,2,0:T(8,128)(2,1)} %copy.169) | copy-start | bytes 786436
  76.7 5.7 copy-start.14
  82.4 28.2 %copy-start.25 = (f32[128]{0:T(128)S(1)}, f32[128]{0:T(128)}, u32[]{:S(2)}) copy-start(f32[128]{0:T(128)} %broadcast_multiply_fusion) | copy-start | bytes 1540
  134.4 65.9 %copy-start.12 = (f32[128,256]{1,0:T(8,128)S(1)}, f32[128,256]{1,0:T(8,128)}, u32[]{:S(2)}) copy-start(f32[128,256]{1,0:T(8,128)} %copy-done.11) | copy-start | bytes 393220
  134.4 65.9 %copy-start.15 = (pred[2048,128]{0,1:T(8,128)(4,1)S(1)}, pred[2048,128]{0,1:T(8,128)(4,1)}, u32[]{:S(2)}) copy-start(pred[2048,128]{0,1:T(8,128)(4,1)} %compare_and_fusion) | copy-start | bytes 786436
  134.4 65.9 %copy-start.16 = (f32[2048,8]{0,1:T(8,128)S(1)}, f32[2048,8]{0,1:T(8,128)}, u32[]{:S(2)}) copy-start(f32[2048,8]{0,1:T(8,128)} %all_gather.22) | copy-start | bytes 196612
  134.4 65.9 %copy-start.17 = (f32[2048,8]{0,1:T(8,128)S(1)}, f32[2048,8]{0,1:T(8,128)}, u32[]{:S(2)}) copy-start(f32[2048,8]{0,1:T(8,128)} %all_gather.24) | copy-start | bytes 196612
  134.4 65.9 %copy-start.26 = (f32[128]{0:T(128)S(1)}, f32[128]{0:T(128)}, u32[]{:S(2)}) copy-start(f32[128]{0:T(128)} %broadcast_multiply_fusion) | copy-start | bytes 1540
  200.4 10.6 copy-start.24
  210.3 821.3 %copy-start.5 = (bf16[1,128,1024]{1,2,0:T(8,128)(2,1)S(1)}, bf16[1,128,1024]{1,2,0:T(8,128)(2,1)}, u32[]{:S(2)}) copy-start(bf16[1,128,1024]{1,2,0:T(8,128)(2,1)} %copy.119) | copy-start | bytes 786436
  210.3 821.3 %copy-start.8 = (pred[128,2048]{0,1:T(8,128)(4,1)S(1)}, pred[128,2048]{0,1:T(8,128)(4,1)}, u32[]{:S(2)}) copy-start(pred[128,2048]{0,1:T(8,128)(4,1)} %copy-done.6) | copy-start | bytes 786436
  898.0 206.4 %copy-start.10 = (bf16[8,128,128]{1,2,0:T(8,128)(2,1)S(1)}, bf16[8,128,128]{1,2,0:T(8,128)(2,1)}, u32[]{:S(2)}) copy-start(bf16[8,128,128]{1,2,0:T(8,128)(2,1)} %copy-done.9) | copy-start | bytes 786436
  899.4 16.4 %collective-permute-start.41 = (bf16[24,256]{1,0:T(8,128)(2,1)}, bf16[24,256]{1,0:T(8,128)(2,1)}, u32[]{:S(2)}, u32[]{:S(2)}) collective-permute-start(bf16[24,256]{1,0:T(8,128)(2,1)} %convert.118), channel_id=1, source_target_pairs={{0,42},{1,43},{2,44},{3,45},{4,46},{5,47},{6,48},{7,49},{8,50},{9,... | collective-permute-start | bytes 36872
  901.3 16.4 %collective-permute-start.40 = (bf16[24,256]{1,0:T(8,128)(2,1)}, bf16[24,256]{1,0:T(8,128)(2,1)}, u32[]{:S(2)}, u32[]{:S(2)}) collective-permute-start(bf16[24,256]{1,0:T(8,128)(2,1)} %convert.118), channel_id=1, source_target_pairs={{0,41},{1,42},{2,43},{3,44},{4,45},{5,46},{6,47},{7,48},{8,49},{9,... | collective-permute-start | bytes 36872
  903.9 10.0 collective-permute-start.42
  910.2 9.4 collective-permute-start.39
  912.0 9.4 collective-permute-start.38
  913.9 9.4 collective-permute-start.37
  915.8 19.4 %collective-permute-start.36 = (bf16[24,256]{1,0:T(8,128)(2,1)}, bf16[24,256]{1,0:T(8,128)(2,1)}, u32[]{:S(2)}, u32[]{:S(2)}) collective-permute-start(bf16[24,256]{1,0:T(8,128)(2,1)} %convert.118), channel_id=1, source_target_pairs={{0,37},{1,38},{2,39},{3,40},{4,41},{5,42},{6,43},{7,44},{8,45},{9,... | collective-permute-start | bytes 36872
  917.7 20.8 %collective-permute-start.35 = (bf16[24,256]{1,0:T(8,128)(2,1)}, bf16[24,256]{1,0:T(8,128)(2,1)}, u32[]{:S(2)}, u32[]{:S(2)}) collective-permute-start(bf16[24,256]{1,0:T(8,128)(2,1)} %convert.118), channel_id=1, source_target_pairs={{0,36},{1,37},{2,38},{3,39},{4,40},{5,41},{6,42},{7,43},{8,44},{9,... | collective-permute-start | bytes 36872
  919.5 21.1 %collective-permute-start.34 = (bf16[24,256]{1,0:T(8,128)(2,1)}, bf16[24,256]{1,0:T(8,128)(2,1)}, u32[]{:S(2)}, u32[]{:S(2)}) collective-permute-start(bf16[24,256]{1,0:T(8,128)(2,1)} %convert.118), channel_id=1, source_target_pairs={{0,35},{1,36},{2,37},{3,38},{4,39},{5,40},{6,41},{7,42},{8,43},{9,... | collective-permute-start | bytes 36872
  921.4 24.9 %collective-permute-start.33 = (bf16[24,256]{1,0:T(8,128)(2,1)}, bf16[24,256]{1,0:T(8,128)(2,1)}, u32[]{:S(2)}, u32[]{:S(2)}) collective-permute-start(bf16[24,256]{1,0:T(8,128)(2,1)} %convert.118), channel_id=1, source_target_pairs={{0,34},{1,35},{2,36},{3,37},{4,38},{5,39},{6,40},{7,41},{8,42},{9,... | collective-permute-start | bytes 36872
  923.3 24.9 %collective-permute-start.32 = (bf16[24,256]{1,0:T(8,128)(2,1)}, bf16[24,256]{1,0:T(8,128)(2,1)}, u32[]{:S(2)}, u32[]{:S(2)}) collective-permute-start(bf16[24,256]{1,0:T(8,128)(2,1)} %convert.118), channel_id=1, source_target_pairs={{0,33},{1,34},{2,35},{3,36},{4,37},{5,38},{6,39},{7,40},{8,41},{9,... | collective-permute-start | bytes 36872
  935.2 14.9 %collective-permute-start.31 = (bf16[24,256]{1,0:T(8,128)(2,1)}, bf16[24,256]{1,0:T(8,128)(2,1)}, u32[]{:S(2)}, u32[]{:S(2)}) collective-permute-start(bf16[24,256]{1,0:T(8,128)(2,1)} %convert.118), channel_id=1, source_target_pairs={{0,32},{1,33},{2,34},{3,35},{4,36},{5,37},{6,38},{7,39},{8,40},{9,... | collective-permute-start | bytes 36872
  938.5 13.5 %collective-permute-start.30 = (bf16[24,256]{1,0:T(8,128)(2,1)}, bf16[24,256]{1,0:T(8,128)(2,1)}, u32[]{:S(2)}, u32[]{:S(2)}) collective-permute-start(bf16[24,256]{1,0:T(8,128)(2,1)} %convert.118), channel_id=1, source_target_pairs={{0,31},{1,32},{2,33},{3,34},{4,35},{5,36},{6,37},{7,38},{8,39},{9,... | collective-permute-start | bytes 36872
  940.7 13.2 %collective-permute-start.29 = (bf16[24,256]{1,0:T(8,128)(2,1)}, bf16[24,256]{1,0:T(8,128)(2,1)}, u32[]{:S(2)}, u32[]{:S(2)}) collective-permute-start(bf16[24,256]{1,0:T(8,128)(2,1)} %convert.118), channel_id=1, source_target_pairs={{0,30},{1,31},{2,32},{3,33},{4,34},{5,35},{6,36},{7,37},{8,38},{9,... | collective-permute-start | bytes 36872
  946.3 11.3 collective-permute-start.28
  948.2 11.9 %collective-permute-start.27 = (bf16[24,256]{1,0:T(8,128)(2,1)}, bf16[24,256]{1,0:T(8,128)(2,1)}, u32[]{:S(2)}, u32[]{:S(2)}) collective-permute-start(bf16[24,256]{1,0:T(8,128)(2,1)} %convert.118), channel_id=1, source_target_pairs={{0,28},{1,29},{2,30},{3,31},{4,32},{5,33},{6,34},{7,35},{8,36},{9,... | collective-permute-start | bytes 36872
  950.1 12.1 %collective-permute-start.26 = (bf16[24,256]{1,0:T(8,128)(2,1)}, bf16[24,256]{1,0:T(8,128)(2,1)}, u32[]{:S(2)}, u32[]{:S(2)}) collective-permute-start(bf16[24,256]{1,0:T(8,128)(2,1)} %convert.118), channel_id=1, source_target_pairs={{0,27},{1,28},{2,29},{3,30},{4,31},{5,32},{6,33},{7,34},{8,35},{9,... | collective-permute-start | bytes 36872
  952.0 12.1 %collective-permute-start.25 = (bf16[24,256]{1,0:T(8,128)(2,1)}, bf16[24,256]{1,0:T(8,128)(2,1)}, u32[]{:S(2)}, u32[]{:S(2)}) collective-permute-start(bf16[24,256]{1,0:T(8,128)(2,1)} %convert.118), channel_id=1, source_target_pairs={{0,26},{1,27},{2,28},{3,29},{4,30},{5,31},{6,32},{7,33},{8,34},{9,... | collective-permute-start | bytes 36872
  953.9 13.6 %collective-permute-start.24 = (bf16[24,256]{1,0:T(8,128)(2,1)}, bf16[24,256]{1,0:T(8,128)(2,1)}, u32[]{:S(2)}, u32[]{:S(2)}) collective-permute-start(bf16[24,256]{1,0:T(8,128)(2,1)} %convert.118), channel_id=1, source_target_pairs={{0,25},{1,26},{2,27},{3,28},{4,29},{5,30},{6,31},{7,32},{8,33},{9,... | collective-permute-start | bytes 36872
  957.6 11.7 %collective-permute-start.23 = (bf16[24,256]{1,0:T(8,128)(2,1)}, bf16[24,256]{1,0:T(8,128)(2,1)}, u32[]{:S(2)}, u32[]{:S(2)}) collective-permute-start(bf16[24,256]{1,0:T(8,128)(2,1)} %convert.118), channel_id=1, source_target_pairs={{0,24},{1,25},{2,26},{3,27},{4,28},{5,29},{6,30},{7,31},{8,32},{9,... | collective-permute-start | bytes 36872
  960.1 11.1 collective-permute-start.22
  962.2 12.8 %collective-permute-start.21 = (bf16[24,256]{1,0:T(8,128)(2,1)}, bf16[24,256]{1,0:T(8,128)(2,1)}, u32[]{:S(2)}, u32[]{:S(2)}) collective-permute-start(bf16[24,256]{1,0:T(8,128)(2,1)} %convert.118), channel_id=1, source_target_pairs={{0,22},{1,23},{2,24},{3,25},{4,26},{5,27},{6,28},{7,29},{8,30},{9,... | collective-permute-start | bytes 36872
  964.1 12.8 %collective-permute-start.20 = (bf16[24,256]{1,0:T(8,128)(2,1)}, bf16[24,256]{1,0:T(8,128)(2,1)}, u32[]{:S(2)}, u32[]{:S(2)}) collective-permute-start(bf16[24,256]{1,0:T(8,128)(2,1)} %convert.118), channel_id=1, source_target_pairs={{0,21},{1,22},{2,23},{3,24},{4,25},{5,26},{6,27},{7,28},{8,29},{9,... | collective-permute-start | bytes 36872
  967.4 11.5 collective-permute-start.19
  969.3 11.7 %collective-permute-start.18 = (bf16[24,256]{1,0:T(8,128)(2,1)}, bf16[24,256]{1,0:T(8,128)(2,1)}, u32[]{:S(2)}, u32[]{:S(2)}) collective-permute-start(bf16[24,256]{1,0:T(8,128)(2,1)} %convert.118), channel_id=1, source_target_pairs={{0,19},{1,20},{2,21},{3,22},{4,23},{5,24},{6,25},{7,26},{8,27},{9,... | collective-permute-start | bytes 36872
  971.2 15.3 %collective-permute-start.17 = (bf16[24,256]{1,0:T(8,128)(2,1)}, bf16[24,256]{1,0:T(8,128)(2,1)}, u32[]{:S(2)}, u32[]{:S(2)}) collective-permute-start(bf16[24,256]{1,0:T(8,128)(2,1)} %convert.118), channel_id=1, source_target_pairs={{0,18},{1,19},{2,20},{3,21},{4,22},{5,23},{6,24},{7,25},{8,26},{9,... | collective-permute-start | bytes 36872
  975.0 13.5 %collective-permute-start.16 = (bf16[24,256]{1,0:T(8,128)(2,1)}, bf16[24,256]{1,0:T(8,128)(2,1)}, u32[]{:S(2)}, u32[]{:S(2)}) collective-permute-start(bf16[24,256]{1,0:T(8,128)(2,1)} %convert.118), channel_id=1, source_target_pairs={{0,17},{1,18},{2,19},{3,20},{4,21},{5,22},{6,23},{7,24},{8,25},{9,... | collective-permute-start | bytes 36872
  977.0 13.4 %collective-permute-start.15 = (bf16[24,256]{1,0:T(8,128)(2,1)}, bf16[24,256]{1,0:T(8,128)(2,1)}, u32[]{:S(2)}, u32[]{:S(2)}) collective-permute-start(bf16[24,256]{1,0:T(8,128)(2,1)} %convert.118), channel_id=1, source_target_pairs={{0,16},{1,17},{2,18},{3,19},{4,20},{5,21},{6,22},{7,23},{8,24},{9,... | collective-permute-start | bytes 36872
  978.9 13.4 %collective-permute-start.14 = (bf16[24,256]{1,0:T(8,128)(2,1)}, bf16[24,256]{1,0:T(8,128)(2,1)}, u32[]{:S(2)}, u32[]{:S(2)}) collective-permute-start(bf16[24,256]{1,0:T(8,128)(2,1)} %convert.118), channel_id=1, source_target_pairs={{0,15},{1,16},{2,17},{3,18},{4,19},{5,20},{6,21},{7,22},{8,23},{9,... | collective-permute-start | bytes 36872
  981.0 15.1 %collective-permute-start.13 = (bf16[24,256]{1,0:T(8,128)(2,1)}, bf16[24,256]{1,0:T(8,128)(2,1)}, u32[]{:S(2)}, u32[]{:S(2)}) collective-permute-start(bf16[24,256]{1,0:T(8,128)(2,1)} %convert.118), channel_id=1, source_target_pairs={{0,14},{1,15},{2,16},{3,17},{4,18},{5,19},{6,20},{7,21},{8,22},{9,... | collective-permute-start | bytes 36872
  986.5 13.1 %collective-permute-start.12 = (bf16[24,256]{1,0:T(8,128)(2,1)}, bf16[24,256]{1,0:T(8,128)(2,1)}, u32[]{:S(2)}, u32[]{:S(2)}) collective-permute-start(bf16[24,256]{1,0:T(8,128)(2,1)} %convert.118), channel_id=1, source_target_pairs={{0,13},{1,14},{2,15},{3,16},{4,17},{5,18},{6,19},{7,20},{8,21},{9,... | collective-permute-start | bytes 36872
  988.5 16.8 %collective-permute-start.11 = (bf16[24,256]{1,0:T(8,128)(2,1)}, bf16[24,256]{1,0:T(8,128)(2,1)}, u32[]{:S(2)}, u32[]{:S(2)}) collective-permute-start(bf16[24,256]{1,0:T(8,128)(2,1)} %convert.118), channel_id=1, source_target_pairs={{0,12},{1,13},{2,14},{3,15},{4,16},{5,17},{6,18},{7,19},{8,20},{9,... | collective-permute-start | bytes 36872
  990.3 28.0 %collective-permute-start.10 = (bf16[24,256]{1,0:T(8,128)(2,1)}, bf16[24,256]{1,0:T(8,128)(2,1)}, u32[]{:S(2)}, u32[]{:S(2)}) collective-permute-start(bf16[24,256]{1,0:T(8,128)(2,1)} %convert.118), channel_id=1, source_target_pairs={{0,11},{1,12},{2,13},{3,14},{4,15},{5,16},{6,17},{7,18},{8,19},{9,... | collective-permute-start | bytes 36872
  992.3 46.8 %collective-permute-start.9 = (bf16[24,256]{1,0:T(8,128)(2,1)}, bf16[24,256]{1,0:T(8,128)(2,1)}, u32[]{:S(2)}, u32[]{:S(2)}) collective-permute-start(bf16[24,256]{1,0:T(8,128)(2,1)} %convert.118), channel_id=1, source_target_pairs={{0,10},{1,11},{2,12},{3,13},{4,14},{5,15},{6,16},{7,17},{8,18},{9,... | collective-permute-start | bytes 36872
  996.1 55.8 %collective-permute-start.8 = (bf16[24,256]{1,0:T(8,128)(2,1)}, bf16[24,256]{1,0:T(8,128)(2,1)}, u32[]{:S(2)}, u32[]{:S(2)}) collective-permute-start(bf16[24,256]{1,0:T(8,128)(2,1)} %convert.118), channel_id=1, source_target_pairs={{0,9},{1,10},{2,11},{3,12},{4,13},{5,14},{6,15},{7,16},{8,17},{9,1... | collective-permute-start | bytes 36872
  999.5 65.5 %collective-permute-start.7 = (bf16[24,256]{1,0:T(8,128)(2,1)}, bf16[24,256]{1,0:T(8,128)(2,1)}, u32[]{:S(2)}, u32[]{:S(2)}) collective-permute-start(bf16[24,256]{1,0:T(8,128)(2,1)} %convert.118), channel_id=1, source_target_pairs={{0,8},{1,9},{2,10},{3,11},{4,12},{5,13},{6,14},{7,15},{8,16},{9,17... | collective-permute-start | bytes 36872
  1005.2 72.9 %collective-permute-start.6 = (bf16[24,256]{1,0:T(8,128)(2,1)}, bf16[24,256]{1,0:T(8,128)(2,1)}, u32[]{:S(2)}, u32[]{:S(2)}) collective-permute-start(bf16[24,256]{1,0:T(8,128)(2,1)} %convert.118), channel_id=1, source_target_pairs={{0,7},{1,8},{2,9},{3,10},{4,11},{5,12},{6,13},{7,14},{8,15},{9,16}... | collective-permute-start | bytes 36872
  1018.4 72.9 %collective-permute-start.5 = (bf16[24,256]{1,0:T(8,128)(2,1)}, bf16[24,256]{1,0:T(8,128)(2,1)}, u32[]{:S(2)}, u32[]{:S(2)}) collective-permute-start(bf16[24,256]{1,0:T(8,128)(2,1)} %convert.118), channel_id=1, source_target_pairs={{0,6},{1,7},{2,8},{3,9},{4,10},{5,11},{6,12},{7,13},{8,14},{9,15},... | collective-permute-start | bytes 36872
  1039.1 69.4 %collective-permute-start.4 = (bf16[24,256]{1,0:T(8,128)(2,1)}, bf16[24,256]{1,0:T(8,128)(2,1)S(1)}, u32[]{:S(2)}, u32[]{:S(2)}) collective-permute-start(bf16[24,256]{1,0:T(8,128)(2,1)} %convert.118), channel_id=1, source_target_pairs={{0,5},{1,6},{2,7},{3,8},{4,9},{5,10},{6,11},{7,12},{8,13},{9,14},{... | collective-permute-start | bytes 36872
  1051.9 56.6 %collective-permute-start.3 = (bf16[24,256]{1,0:T(8,128)(2,1)}, bf16[24,256]{1,0:T(8,128)(2,1)S(1)}, u32[]{:S(2)}, u32[]{:S(2)}) collective-permute-start(bf16[24,256]{1,0:T(8,128)(2,1)} %convert.118), channel_id=1, source_target_pairs={{0,4},{1,5},{2,6},{3,7},{4,8},{5,9},{6,10},{7,11},{8,12},{9,13},{1... | collective-permute-start | bytes 36872
  1065.1 43.5 %collective-permute-start.2 = (bf16[24,256]{1,0:T(8,128)(2,1)}, bf16[24,256]{1,0:T(8,128)(2,1)S(1)}, u32[]{:S(2)}, u32[]{:S(2)}) collective-permute-start(bf16[24,256]{1,0:T(8,128)(2,1)} %convert.118), channel_id=1, source_target_pairs={{0,3},{1,4},{2,5},{3,6},{4,7},{5,8},{6,9},{7,10},{8,11},{9,12},{10... | collective-permute-start | bytes 36872
  1078.2 30.3 %collective-permute-start.1 = (bf16[24,256]{1,0:T(8,128)(2,1)}, bf16[24,256]{1,0:T(8,128)(2,1)S(1)}, u32[]{:S(2)}, u32[]{:S(2)}) collective-permute-start(bf16[24,256]{1,0:T(8,128)(2,1)} %convert.118), channel_id=1, source_target_pairs={{0,2},{1,3},{2,4},{3,5},{4,6},{5,7},{6,8},{7,9},{8,10},{9,11},{10,... | collective-permute-start | bytes 36872
  1091.3 18.4 %collective-permute-start = (bf16[24,256]{1,0:T(8,128)(2,1)}, bf16[24,256]{1,0:T(8,128)(2,1)}, u32[]{:S(2)}, u32[]{:S(2)}) collective-permute-start(bf16[24,256]{1,0:T(8,128)(2,1)} %convert.118), channel_id=1, source_target_pairs={{0,1},{1,2},{2,3},{3,4},{4,5},{5,6},{6,7},{7,8},{8,9},{9,10},{10,1... | collective-permute-start | bytes 36872
  (9 other events, 19.5 us)
Sparse Core Ops, SparseCore 0:
  12.4 50.2 all-gather.5
  65.7 62.0 all-gather.7
  130.7 62.1 all-gather.9
where the time goes:
time: 1160 us; the launch traced here: 1150 us
  blocking collectives  753 us (65%)
  starting transfers between devices  197 us (17%)
  waiting for transfers between devices  74.4 us (6%)
  matrix products  52 us (4%)
  local copies, waits for them, and re-layouts  49.3 us (4%)
  between operations  14.3 us (1%)
  other arithmetic  12.3 us (1%)
    unnamed x1, blocking collectives  681 us
    unnamed x43, starting transfers between devices  197 us
    all_gather x1, waiting for transfers between devices, per_device(): grad_part = lax.all_gather(out_grad[0], 'cp', axis=0, tiled=True)  58.5 us
    unnamed x59, local copies, waits for them, and re-layouts  46.9 us
    all_gather x1, blocking collectives, per_device(): lax.all_gather(row_delta.T, 'cp', axis=0, tiled=True)  24.9 us
    all_gather x1, blocking collectives, per_device(): lax.all_gather(clean_kv[:, :head_size], 'cp', axis=0, tiled=True)  24.1 us
  transfers between devices with their start and end apart: 46, of which 2 were waited for; matrix products, arithmetic and copies ran while one was open for 4% of the time, Pallas kernels for 0%

commit v1 on v0

v1 whole, which is shorter than its diff:
```python
import functools

import jax
import jax.numpy as jnp
from jax import lax
from jax.experimental import pallas as pl
from jax.experimental.pallas import tpu as pltpu
from jax.sharding import Mesh
from jax.sharding import PartitionSpec as P

BLK = 64
EPSILON = 1e-06
NEGATIVE = -1e30
VMEM_LIMIT = 56 * 1024 * 1024

F32 = jnp.float32
BF16 = jnp.bfloat16


def project_kernel(
    cp_ref, len_ref, cplace_ref, nplace_ref, clean_ref, noisy_ref, w_ref, gain_ref,
    spread_ref, nkv_ref, pre_ref, bias_ref, acc_ref,
):
    step = pl.program_id(0)
    rows, hd = clean_ref.shape[0], gain_ref.shape[1]
    hidden = jnp.concatenate([clean_ref[...], noisy_ref[...]], axis=0)
    part = jnp.dot(hidden, w_ref[...], preferred_element_type=F32)

    @pl.when(step == 0)
    def _():
        acc_ref[...] = part
        blocks, docs = cplace_ref.shape[1], len_ref.shape[1]
        keys = blocks * BLK
        logical, starts = [], []
        for local in range(rows // BLK):
            slot = cp_ref[0, 0] * (rows // BLK) + local
            log = jnp.int32(0)
            for b in range(blocks):
                log = log + jnp.where(nplace_ref[0, b] == slot, b, 0)
            end, start = jnp.int32(0), jnp.int32(0)
            for d in range(docs):
                end = end + len_ref[0, d]
                start = jnp.where(end <= log, end, start)
            logical.append(log)
            starts.append(start)
        row = lax.broadcasted_iota(jnp.int32, (8, keys), 0)
        slots = lax.broadcasted_iota(jnp.int32, (8, keys), 1) // BLK
        key_log = jnp.zeros((8, keys), jnp.int32)
        for b in range(blocks):
            key_log = jnp.where(slots == cplace_ref[0, b], b, key_log)
        low = jnp.where(row == 0, starts[0], starts[1])
        high = jnp.where(row == 0, logical[0], logical[1])
        bias_ref[:, :keys] = jnp.where((key_log >= low) & (key_log < high), 0.0, NEGATIVE)
        own = lax.broadcasted_iota(jnp.int32, (8, rows), 1) // BLK
        bias_ref[:, keys:] = jnp.where(
            own == lax.broadcasted_iota(jnp.int32, (8, rows), 0), 0.0, NEGATIVE
        )

    @pl.when(step > 0)
    def _():
        acc_ref[...] += part

    @pl.when(step == pl.num_programs(0) - 1)
    def _():
        pre = acc_ref[:, :hd]
        inverse = lax.rsqrt(jnp.mean(pre * pre, axis=1, keepdims=True) + EPSILON)
        keys = (pre * inverse * gain_ref[...]).astype(BF16)
        values = acc_ref[:, hd:].astype(BF16)
        pre_ref[...] = pre
        nkv_ref[:, :hd] = keys[rows:]
        nkv_ref[:, hd:] = values[rows:]
        for dest in range(spread_ref.shape[0]):
            spread_ref[dest, :, :hd] = keys[:rows]
            spread_ref[dest, :, hd:] = values[:rows]


def attention_kernel(
    q_ref, do_ref, ckv_ref, nkv_ref, bias_ref,
    out_ref, dq_ref, dkv_ref, dnkv_ref,
    k_ref, v_ref, mask_ref, qs_ref, dos_ref, p_ref, ds_ref,
):
    tok, heads = q_ref.shape[0], q_ref.shape[1] // 128
    hd = 128
    scale = hd ** (-0.5)
    peers = ckv_ref.shape[0]
    for c in range(peers):
        k_ref[c * tok : (c + 1) * tok, :] = ckv_ref[c, :, :hd]
        v_ref[c * tok : (c + 1) * tok, :] = ckv_ref[c, :, hd:]
    k_ref[peers * tok :, :] = nkv_ref[:, :hd]
    v_ref[peers * tok :, :] = nkv_ref[:, hd:]
    total = k_ref.shape[0]
    for local in range(tok // BLK):
        mask_ref[local * BLK : (local + 1) * BLK, :] = jnp.broadcast_to(
            bias_ref[local : local + 1, :], (BLK, total)
        )
    for h in range(heads):
        qs_ref[h * tok : (h + 1) * tok, :] = q_ref[:, h * hd : (h + 1) * hd]
        dos_ref[h * tok : (h + 1) * tok, :] = do_ref[:, h * hd : (h + 1) * hd]

    def one_head(h, carry):
        at = pl.ds(pl.multiple_of(h * tok, tok), tok)
        cols = pl.ds(pl.multiple_of(h * hd, hd), hd)
        q, do = qs_ref[at, :], dos_ref[at, :]
        s = lax.dot_general(q, k_ref[...], (((1,), (1,)), ((), ())), preferred_element_type=F32)
        s = s * scale + mask_ref[...]
        e = jnp.exp(s - jnp.max(s, axis=1, keepdims=True))
        p = e * (1.0 / jnp.sum(e, axis=1, keepdims=True))
        p_low = p.astype(BF16)
        p_ref[at, :] = p_low
        out = jnp.dot(p_low, v_ref[...], preferred_element_type=F32).astype(BF16)
        out_ref[:, cols] = out
        delta = jnp.sum(do.astype(F32) * out.astype(F32), axis=1, keepdims=True)
        dp = lax.dot_general(do, v_ref[...], (((1,), (1,)), ((), ())), preferred_element_type=F32)
        ds = (p * (dp - delta)).astype(BF16)
        ds_ref[at, :] = ds
        dq = jnp.dot(ds, k_ref[...], preferred_element_type=F32) * scale
        dq_ref[:, cols] = dq.astype(BF16)
        return carry

    lax.fori_loop(0, heads, one_head, 0)
    q_t = qs_ref[...].T
    do_t = dos_ref[...].T

    def one_peer(c, carry):
        cols = pl.ds(pl.multiple_of(c * tok, tok), tok)
        dk = jnp.dot(q_t, ds_ref[:, cols], preferred_element_type=F32) * scale
        dv = jnp.dot(do_t, p_ref[:, cols], preferred_element_type=F32)
        dkv_ref[c, :hd, :] = dk.astype(BF16)
        dkv_ref[c, hd:, :] = dv.astype(BF16)
        return carry

    lax.fori_loop(0, peers, one_peer, 0)
    dnkv_ref[:hd, :] = jnp.dot(q_t, ds_ref[:, peers * tok :], preferred_element_type=F32) * scale
    dnkv_ref[hd:, :] = jnp.dot(do_t, p_ref[:, peers * tok :], preferred_element_type=F32)


def weight_kernel(
    core_ref, recv_ref, dnkv_ref, pre_ref, gain_ref, clean_ref, noisy_ref,
    send_ref, keep_ref, g_ref, dw_ref,
):
    step = pl.program_id(0)
    rows, hd = clean_ref.shape[0], gain_ref.shape[1]
    width = clean_ref.shape[1]
    half = width // 2
    peers, per = send_ref.shape[0], send_ref.shape[1]

    @pl.when(step == 0)
    def _():
        summed = recv_ref[0].astype(F32)
        for c in range(1, recv_ref.shape[0]):
            summed = summed + recv_ref[c].astype(F32)
        for copy, grad_t in enumerate((summed, dnkv_ref[...])):
            at = slice(copy * rows, (copy + 1) * rows)
            pre = pre_ref[at, :]
            inverse = lax.rsqrt(jnp.mean(pre * pre, axis=1, keepdims=True) + EPSILON)
            scaled = grad_t[:hd].T * gain_ref[...]
            inner = jnp.mean(scaled * pre, axis=1, keepdims=True)
            pre_grad = inverse * scaled - pre * inverse * inverse * inverse * inner
            g_ref[at, :hd] = pre_grad.astype(BF16)
            g_ref[at, hd:] = grad_t[hd:].T.astype(BF16)

    hidden = jnp.concatenate([clean_ref[...], noisy_ref[...]], axis=0)
    term = lax.dot_general(
        hidden, g_ref[...], (((0,), (0,)), ((), ())), preferred_element_type=F32
    )
    at = pl.ds(pl.multiple_of(step * half, half), half)
    for core in range(2):
        for lane in range(2):
            dw_ref[core, lane, at, :] = term[
                core * half : (core + 1) * half, lane * 128 : (lane + 1) * 128
            ]

    @pl.when(step == pl.num_programs(0) - 1)
    def _():
        mine = core_ref[0, 0]
        zs = pl.num_programs(0)

        def one_peer(j, carry):
            for ref, core in ((send_ref, 1 - mine), (keep_ref, mine)):
                for i in range(per):
                    for lane in range(2):
                        piece = dw_ref[core, lane, pl.ds(j * per + i, 8, stride=half), :]
                        ref[j, i, :, lane * 128 : (lane + 1) * 128] = piece.astype(BF16)
            return carry

        lax.fori_loop(0, peers, one_peer, 0)


def per_device(
    clean_hidden, noisy_hidden, noisy_query, out_grad, kv_weight, key_gain,
    doc_lengths, clean_place, noisy_place,
):
    rows, width = clean_hidden.shape[1:]
    hd = key_gain.shape[0]
    peers = lax.axis_size(("y", "x"))
    zs = lax.axis_size("z")
    blocks = clean_place.shape[1]
    keys = blocks * BLK
    total = keys + rows
    heads = noisy_query.shape[2] // hd
    clean, noisy = clean_hidden[0], noisy_hidden[0]
    gain = key_gain.reshape(1, hd)
    cp_index = lax.axis_index(("y", "x")).reshape(1, 1).astype(jnp.int32)
    core_index = lax.axis_index("core").reshape(1, 1).astype(jnp.int32)
    smem = pl.BlockSpec(memory_space=pltpu.SMEM)
    params = pltpu.CompilerParams(vmem_limit_bytes=VMEM_LIMIT)

    def whole(*shape):
        return pl.BlockSpec(shape, lambda *_: (0,) * len(shape))

    steps = 5
    part = width // steps
    spread, nkv, pre, bias = pl.pallas_call(
        project_kernel,
        grid=(steps,),
        in_specs=[smem, smem, smem, smem]
        + [pl.BlockSpec((rows, part), lambda s: (0, s))] * 2
        + [pl.BlockSpec((part, 2 * hd), lambda s: (s, 0)), whole(1, hd)],
        out_specs=[
            whole(peers, rows, 2 * hd),
            whole(rows, 2 * hd),
            whole(2 * rows, hd),
            whole(8, total),
        ],
        out_shape=[
            jax.ShapeDtypeStruct((peers, rows, 2 * hd), BF16),
            jax.ShapeDtypeStruct((rows, 2 * hd), BF16),
            jax.ShapeDtypeStruct((2 * rows, hd), F32),
            jax.ShapeDtypeStruct((8, total), F32),
        ],
        scratch_shapes=[pltpu.VMEM((2 * rows, 2 * hd), F32)],
        compiler_params=params,
        name="project",
    )(cp_index, doc_lengths, clean_place, noisy_place, clean, noisy, kv_weight, gain)

    gathered = lax.all_to_all(spread, ("y", "x"), 0, 0, tiled=True)

    attention, query_grad, dkv, dnkv = pl.pallas_call(
        attention_kernel,
        out_shape=[
            jax.ShapeDtypeStruct((rows, heads * hd), BF16),
            jax.ShapeDtypeStruct((rows, heads * hd), BF16),
            jax.ShapeDtypeStruct((peers, 2 * hd, rows), BF16),
            jax.ShapeDtypeStruct((2 * hd, rows), F32),
        ],
        scratch_shapes=[
            pltpu.VMEM((total, hd), BF16),
            pltpu.VMEM((total, hd), BF16),
            pltpu.VMEM((rows, total), F32),
            pltpu.VMEM((heads * rows, hd), BF16),
            pltpu.VMEM((heads * rows, hd), BF16),
            pltpu.VMEM((heads * rows, total), BF16),
            pltpu.VMEM((heads * rows, total), BF16),
        ],
        compiler_params=params,
        name="attend",
    )(noisy_query[0], out_grad[0], gathered, nkv, bias)

    received = lax.all_to_all(dkv, ("y", "x"), 0, 0, tiled=True)

    slab = width // zs
    per = slab // (2 * peers)
    piece = jax.ShapeDtypeStruct((peers, per, zs, 2 * hd), BF16)
    send, keep = pl.pallas_call(
        weight_kernel,
        grid=(zs,),
        in_specs=[
            smem,
            whole(peers, 2 * hd, rows),
            whole(2 * hd, rows),
            whole(2 * rows, hd),
            whole(1, hd),
        ]
        + [pl.BlockSpec((rows, slab), lambda s: (0, s))] * 2,
        out_specs=[whole(peers, per, zs, 2 * hd)] * 2,
        out_shape=[piece, piece],
        scratch_shapes=[
            pltpu.VMEM((2 * rows, 2 * hd), BF16),
            pltpu.VMEM((2, 2, zs * slab // 2, 128), F32),
        ],
        compiler_params=params,
        name="weight",
    )(core_index, received, dnkv, pre, gain, clean, noisy)

    other = lax.ppermute(send, "core", [(0, 1), (1, 0)])
    both = (keep.astype(F32) + other.astype(F32)).astype(BF16)
    both = lax.all_to_all(both, ("y", "x"), 0, 0, tiled=True)
    term = jnp.sum(both.astype(F32), axis=0).astype(BF16)
    term = lax.all_to_all(jnp.swapaxes(term, 0, 1), "z", 0, 0, tiled=True)
    share = jnp.sum(term.astype(F32), axis=0).astype(BF16)
    return (attention[None], query_grad[None], share)


def solution(mesh):
    zs, cps = mesh.devices.shape[0] // 2, mesh.devices.shape[1]
    side = int(round(cps**0.5))
    grid = Mesh(mesh.devices.reshape(zs, 2, cps // side, side), ("z", "core", "y", "x"))
    grp, cp = ("z", "core"), ("y", "x")
    in_specs = (
        P(grp, cp, None),
        P(grp, cp, None),
        P(grp, cp, None),
        P(grp, cp, None),
        P(),
        P(),
        P(grp, None),
        P(grp, None),
        P(grp, None),
    )
    out_specs = (P(grp, cp, None), P(grp, cp, None), P(grp + cp, None))
    return jax.shard_map(
        per_device, mesh=grid, in_specs=in_specs, out_specs=out_specs, check_vma=False
    )
```

time: 1160 us -> 128 us (0.11)
  blocking collectives: 753 us -> 63.5 us
  starting transfers between devices: 197 us -> 4.9 us
  waiting for transfers between devices: 74.4 us -> 18.5 us
  matrix products: 52 us -> 0 us
  local copies, waits for them, and re-layouts: 49.3 us -> 1 us
  Pallas kernels: 0 us -> 35.9 us
  between operations: 14.3 us -> 0.66 us
    unnamed x1 -> x0, blocking collectives: 681 us -> none
    unnamed x43 -> x0, starting transfers between devices: 197 us -> none
    all_gather x3 -> x0, waiting for transfers between devices: 74.2 us -> none  [the longest x1 58.5 us: per_device(): grad_part = lax.all_gather(out_grad[0], 'cp', axis=0, tiled=True)]
    all_gather x3 -> x0, blocking collectives: 72.1 us -> none  [the longest x1 24.9 us: per_device(): lax.all_gather(row_delta.T, 'cp', axis=0, tiled=True)]
    all_to_all x0 -> x3, blocking collectives: none -> 63.5 us  [the longest x1 23.4 us: per_device(): gathered = lax.all_to_all(spread, ('y', 'x'), 0, 0, tiled=True)]
    dot_general x16 -> x0, matrix products: 52 us -> none  [the longest x4 12.7 us: scores(): jnp.einsum('rhd,kd->hrk', queries, key_rows, preferred_element_type=jnp.f...]
    unnamed x59 -> x2, local copies, waits for them, and re-layouts: 46.9 us -> 0.98 us
    pallas_call x0 -> x3, Pallas kernels: none -> 35.9 us  [the longest x1 18.3 us: per_device(): pl.pallas_call(attention_kernel, out_shape=[jax.ShapeDtypeStruct((rows, h...]
  transfers between devices with their start and end apart: 46 -> 2, of which waited for: 2 -> 2; matrix products, arithmetic and copies ran while one was open for 4% -> 0% of each run, Pallas kernels for 0% -> 0%
where the time goes in v1:
time: 128 us; the launch traced here: 127 us
  blocking collectives  63.5 us (50%)
  Pallas kernels  35.9 us (28%)
  waiting for transfers between devices  18.5 us (14%)
  starting transfers between devices  4.9 us (4%)
  other arithmetic  2.53 us (2%)
    all_to_all x1, blocking collectives, per_device(): gathered = lax.all_to_all(spread, ('y', 'x'), 0, 0, tiled=True)  23.4 us
    all_to_all x1, blocking collectives, per_device(): both = lax.all_to_all(both, ('y', 'x'), 0, 0, tiled=True)  23.2 us
    pallas_call x1, Pallas kernels, per_device(): pl.pallas_call(attention_kernel, out_shape=[jax.ShapeDtypeStruct((rows, h...  18.3 us
    all_to_all x1, blocking collectives, per_device(): term = lax.all_to_all(jnp.swapaxes(term, 0, 1), 'z', 0, 0, tiled=True)  17 us
    all_to_all x1, waiting for transfers between devices, per_device(): received = lax.all_to_all(dkv, ('y', 'x'), 0, 0, tiled=True)  15.2 us
    pallas_call x1, Pallas kernels, per_device(): pl.pallas_call(weight_kernel, grid=(zs,), in_specs=[smem, whole(peers, 2...  11.3 us
    pallas_call x1, Pallas kernels, per_device(): pl.pallas_call(project_kernel, grid=(steps,), in_specs=[smem, smem, smem,...  6.24 us
    all_to_all x1, starting transfers between devices, per_device(): received = lax.all_to_all(dkv, ('y', 'x'), 0, 0, tiled=True)  4.9 us
  transfers between devices with their start and end apart: 2, of which 2 were waited for; matrix products, arithmetic and copies ran while one was open for 0% of the time, Pallas kernels for 0%

profile of v1, /device:TPU:2, one launch (start us, length us, event | category | flops | bytes accessed | tf_op | source)
XLA Modules:
  0.0 126.9 jit_solution(504928219095774987)
XLA Ops:
  0.6 6.2 %project.1 = (bf16[16,128,256]{2,1,0:T(8,128)(2,1)}, bf16[128,256]{1,0:T(8,128)(2,1)}, f32[256,128]{1,0:T(8,128)}, f32[8,2176]{1,0:T(8,128)}) custom-call(s32[1,1]{1,0:T(1,128)} %bitcast.2.cp_ref, s32[1,4]{1,0:T(1,128)} %len_ref.1, s32[1,32]{1,0:T(1,128)} %cplace_ref.1, s32[1,32]{1,0:T(1,128)} %nplace_ref.1, bf16[128,5120]{1,0:T(8,128)(2,1)} %bitcast.10, ...), custom_call_target="tpu_custom_call" | custom-call | tf_op jit(solution)/shard_map/project/pallas_call | solution.py:213
  6.9 23.4 %all_to_all.20.ckv_ref = bf16[16,128,256]{2,1,0:T(8,128)(2,1)} all-to-all(bf16[16,128,256]{2,1,0:T(8,128)(2,1)} %get-tuple-element.13), channel_id=1, replica_groups=mesh['z'=8,'core'=2,'y'=4,'x'=4] {'y','x'}, dimensions={0} | all-to-all | bytes 2097152 | tf_op jit(solution)/shard_map/all_to_all | solution.py:236
  30.2 18.3 %attend.1 = (bf16[128,1024]{1,0:T(8,128)(2,1)}, bf16[128,1024]{1,0:T(8,128)(2,1)}, bf16[16,256,128]{2,1,0:T(8,128)(2,1)}, f32[256,128]{1,0:T(8,128)}) custom-call(bf16[128,1024]{1,0:T(8,128)(2,1)} %bitcast.15, bf16[128,1024]{1,0:T(8,128)(2,1)} %bitcast.16, bf16[16,128,256]{2,1,0:T(8,128)(2,1)} %all_to_all.20.ckv_ref, ...), custom_call_target="tpu_custom_call" | custom-call | tf_op jit(solution)/shard_map/attend/pallas_call | solution.py:238
  48.6 4.9 %all-to-all-start.1 = ((bf16[16,256,128]{2,1,0:T(8,128)(2,1)}), bf16[16,256,128]{2,1,0:T(8,128)(2,1)S(1)}, u32[]{:S(2)}, u32[]{:S(2)}) async-start(bf16[16,256,128]{2,1,0:T(8,128)(2,1)} %get-tuple-element.18), calls=%async_computation.1 | async-start | bytes 2097152 | tf_op jit(solution)/shard_map/all_to_all | solution.py:259
  53.5 15.2 %all-to-all-done.1.recv_ref = bf16[16,256,128]{2,1,0:T(8,128)(2,1)S(1)} async-done(((bf16[16,256,128]{2,1,0:T(8,128)(2,1)}), bf16[16,256,128]{2,1,0:T(8,128)(2,1)S(1)}, u32[]{:S(2)}, u32[]{:S(2)}) %all-to-all-start.1) | async-done | bytes 1048608 | tf_op jit(solution)/shard_map/all_to_all | solution.py:259
  68.7 0.0 copy-start
  68.7 1.0 copy-done
  69.7 11.3 %weight.1 = (bf16[16,20,8,256]{3,2,1,0:T(8,128)(2,1)}, bf16[16,20,8,256]{3,2,1,0:T(8,128)(2,1)}) custom-call(s32[1,1]{1,0:T(1,128)} %bitcast.8.core_ref, bf16[16,256,128]{2,1,0:T(8,128)(2,1)} %copy-done, f32[256,128]{1,0:T(8,128)} %get-tuple-element.19.dnkv_ref, f32[256,128]{1,0:T(8,128)} %get-tuple-element.20.pre_ref, f32[1,128]{1,0:T(1,128)} %bitcast.18, ...), custom_call_target="tpu_custom_call" | custom-call | tf_op jit(solution)/shard_map/weight/pallas_call | solution.py:264
  81.0 0.0 collective-permute-start
  81.0 3.2 %collective-permute-done = bf16[16,20,8,256]{3,2,1,0:T(8,128)(2,1)S(1)} collective-permute-done((bf16[16,20,8,256]{3,2,1,0:T(8,128)(2,1)}, bf16[16,20,8,256]{3,2,1,0:T(8,128)(2,1)S(1)}, u32[]{:S(2)}, u32[]{:S(2)}) %collective-permute-start) | collective-permute-done | bytes 1310752 | tf_op jit(solution)/shard_map/ppermute | solution.py:285
  84.2 1.7 %add_convert_fusion = bf16[16,20,8,256]{3,2,1,0:T(8,128)(2,1)S(1)} fusion(bf16[16,20,8,256]{3,2,1,0:T(8,128)(2,1)S(1)} %collective-permute-done, bf16[16,20,8,256]{3,2,1,0:T(8,128)(2,1)} %get-tuple-element.21), kind=kLoop, calls=%fused_computation | loop fusion | flops 2621440 | bytes 3932160 | tf_op jit(solution)/shard_map/convert_element_type | solution.py:286
  85.9 23.2 %all_to_all.21 = bf16[16,20,8,256]{3,2,1,0:T(8,128)(2,1)S(1)} all-to-all(bf16[16,20,8,256]{3,2,1,0:T(8,128)(2,1)S(1)} %add_convert_fusion), channel_id=1, replica_groups=mesh['z'=8,'core'=2,'y'=4,'x'=4] {'y','x'}, dimensions={0} | all-to-all | bytes 2621440 | tf_op jit(solution)/shard_map/all_to_all | solution.py:287
  109.1 0.2 reduce_sum.24
  109.3 17.0 %all_to_all.22 = bf16[8,20,256]{2,1,0:T(8,128)(2,1)S(1)} all-to-all(bf16[8,20,256]{2,1,0:T(8,128)(2,1)S(1)} %copy.12), channel_id=1, replica_groups=mesh['z'=8,'core'=2,'y'=4,'x'=4] {'z'}, dimensions={0} | all-to-all | bytes 163840 | tf_op jit(solution)/shard_map/all_to_all | solution.py:289
  126.3 0.6 reduce_sum.25
  (1 shorter events, 0.0 us)
Async XLA Ops:
  48.6 20.1 %all-to-all-start.1 = ((bf16[16,256,128]{2,1,0:T(8,128)(2,1)}), bf16[16,256,128]{2,1,0:T(8,128)(2,1)S(1)}, u32[]{:S(2)}, u32[]{:S(2)}) async-start(bf16[16,256,128]{2,1,0:T(8,128)(2,1)} %get-tuple-element.18), calls=%async_computation.1 | async-start | bytes 2097152 | tf_op jit(solution)/shard_map/all_to_all | solution.py:259
  68.7 1.0 copy-start
  81.0 3.2 %collective-permute-start = (bf16[16,20,8,256]{3,2,1,0:T(8,128)(2,1)}, bf16[16,20,8,256]{3,2,1,0:T(8,128)(2,1)S(1)}, u32[]{:S(2)}, u32[]{:S(2)}) collective-permute-start(bf16[16,20,8,256]{3,2,1,0:T(8,128)(2,1)} %get-tuple-element.22), channel_id=1, source_target_pairs={{0,16},{16,0},{1,17},{17,1},{2,18},{18,2},{3,19},{19,3},{4,20},{20... | collective-permute-start | bytes 3932168 | tf_op jit(solution)/shard_map/ppermute | solution.py:285

commit v2 on v1

v2 whole, which is shorter than its diff:
```python
import jax
import jax.numpy as jnp
from jax import lax
from jax.experimental import pallas as pl
from jax.experimental.pallas import tpu as pltpu
from jax.sharding import Mesh
from jax.sharding import PartitionSpec as P

BLK = 64
EPSILON = 1e-06
NEGATIVE = -1e30
MIB = 1024 * 1024
LOG2E = 1.4426950408889634

F32 = jnp.float32
BF16 = jnp.bfloat16


def keys_values(joined, gain):
    hd = gain.shape[1]
    pre = joined[:, :hd]
    inverse = lax.rsqrt(jnp.mean(pre * pre, axis=1, keepdims=True) + EPSILON)
    return pre, (pre * inverse * gain).astype(BF16), joined[:, hd:].astype(BF16)


def accumulate(acc_ref, part):
    step = pl.program_id(0)

    @pl.when(step == 0)
    def _():
        acc_ref[...] = part

    @pl.when(step > 0)
    def _():
        acc_ref[...] += part


def clean_kernel(clean_ref, w_ref, gain_ref, spread_ref, pre_ref, acc_ref):
    hd = gain_ref.shape[1]
    accumulate(acc_ref, jnp.dot(clean_ref[...], w_ref[...], preferred_element_type=F32))

    @pl.when(pl.program_id(0) == pl.num_programs(0) - 1)
    def _():
        pre, keys, values = keys_values(acc_ref[...], gain_ref[...])
        pre_ref[...] = pre
        for dest in range(spread_ref.shape[0]):
            spread_ref[dest, :, :hd] = keys
            spread_ref[dest, :, hd:] = values


def prepare_kernel(
    cp_ref, core_ref, len_ref, cplace_ref, nplace_ref, clean_ref, noisy_ref, w_ref, gain_ref,
    nkv_ref, pre_ref, mask_ref, mine_ref, other_ref, acc_ref, turned_ref,
):
    step = pl.program_id(0)
    rows, hd = noisy_ref.shape[0], gain_ref.shape[1]
    half = noisy_ref.shape[1] // 2
    peers, per = mine_ref.shape[0], mine_ref.shape[1]
    accumulate(acc_ref, jnp.dot(noisy_ref[...], w_ref[...], preferred_element_type=F32))
    turned = jnp.concatenate([clean_ref[...], noisy_ref[...]], axis=0).T.astype(F32)
    at = pl.ds(pl.multiple_of(step * half, half), half)
    for core in range(2):
        for lane in range(2):
            turned_ref[core, lane, at, :] = turned[
                core * half : (core + 1) * half, lane * 128 : (lane + 1) * 128
            ]

    @pl.when(step == 0)
    def _():
        blocks, docs = cplace_ref.shape[1], len_ref.shape[1]
        locals_ = rows // BLK
        logical, starts = [], []
        for local in range(locals_):
            slot = cp_ref[0, 0] * locals_ + local
            log = jnp.int32(0)
            for b in range(blocks):
                log = log + jnp.where(nplace_ref[0, b] == slot, b, 0)
            end, start = jnp.int32(0), jnp.int32(0)
            for d in range(docs):
                end = end + len_ref[0, d]
                start = jnp.where(end <= log, end, start)
            logical.append(log)
            starts.append(start)
        lane = lax.broadcasted_iota(jnp.int32, (BLK, hd), 1)
        for b in range(blocks):
            tile = jnp.zeros((BLK, hd), F32)
            for local in range(locals_):
                hidden = jnp.where((starts[local] <= b) & (b < logical[local]), 0.0, NEGATIVE)
                tile = jnp.where(lane == local, hidden, tile)
            slot = pl.multiple_of(cplace_ref[0, b] * BLK, BLK)
            mask_ref[pl.ds(slot, BLK), :] = tile.astype(BF16)
        for local in range(locals_):
            tile = jnp.where((lane < locals_) & (lane != local), NEGATIVE, 0.0)
            first = blocks * BLK + local * BLK
            mask_ref[first : first + BLK, :] = tile.astype(BF16)

    @pl.when(step == pl.num_programs(0) - 1)
    def _():
        pre, keys, values = keys_values(acc_ref[...], gain_ref[...])
        pre_ref[...] = pre
        nkv_ref[:, :hd] = keys
        nkv_ref[:, hd:] = values
        core = core_ref[0, 0]

        def one_peer(j, carry):
            for ref, side in ((other_ref, 1 - core), (mine_ref, core)):
                for i in range(per):
                    for lane in range(2):
                        piece = turned_ref[side, lane, pl.ds(j * per + i, 8, stride=half), :]
                        ref[j, i, :, lane * 128 : (lane + 1) * 128] = piece.astype(BF16)
            return carry

        lax.fori_loop(0, peers, one_peer, 0)


def attention_kernel(
    q_ref, do_ref, ckv_ref, nkv_ref, mask_ref,
    out_ref, dq_ref, dkv_ref, dnkv_ref,
    kx_ref, vx_ref, qx_ref, dox_ref, e_ref, p_ref, ds_ref,
):
    hd = 128
    tok, heads = q_ref.shape[0], q_ref.shape[1] // hd
    scale = hd ** (-0.5)
    peers = ckv_ref.shape[0]
    total = kx_ref.shape[0]
    for c in range(peers):
        kx_ref[c * tok : (c + 1) * tok, :hd] = ckv_ref[c, :, :hd]
        vx_ref[c * tok : (c + 1) * tok, :hd] = ckv_ref[c, :, hd:]
    kx_ref[peers * tok :, :hd] = nkv_ref[:, :hd]
    vx_ref[peers * tok :, :hd] = nkv_ref[:, hd:]
    kx_ref[:, hd:] = mask_ref[...]
    vx_ref[:, hd:] = jnp.ones((total, hd), BF16)
    lane = lax.broadcasted_iota(jnp.int32, (tok, hd), 1)
    block = lax.broadcasted_iota(jnp.int32, (tok, hd), 0) // BLK
    pick = jnp.where(lane == block, 1.0, 0.0).astype(BF16)
    for h in range(heads):
        at = slice(h * tok, (h + 1) * tok)
        qx_ref[at, :hd] = q_ref[:, h * hd : (h + 1) * hd]
        qx_ref[at, hd:] = pick

    def transposed(a, b):
        return lax.dot_general(a, b, (((1,), (1,)), ((), ())), preferred_element_type=F32)

    group = 2 * tok

    def weigh(g, carry):
        at = pl.ds(pl.multiple_of(g * group, group), group)
        s = transposed(qx_ref[at, :], kx_ref[...])
        e = jnp.exp2((s - jnp.max(s, axis=1, keepdims=True)) * (scale * LOG2E))
        e_ref[at, :] = e
        p_ref[at, :] = e.astype(BF16)
        return carry

    lax.fori_loop(0, heads * tok // group, weigh, 0)
    for h in range(heads):
        at, cols = slice(h * tok, (h + 1) * tok), slice(h * hd, (h + 1) * hd)
        o = jnp.dot(p_ref[at, :], vx_ref[...], preferred_element_type=F32)
        over = 1.0 / o[:, hd:]
        out = (o[:, :hd] * over).astype(BF16)
        out_ref[:, cols] = out
        do = (do_ref[:, cols].astype(F32) * over).astype(BF16)
        delta = jnp.sum(do.astype(F32) * out.astype(F32), axis=1, keepdims=True)
        high = delta.astype(BF16).astype(F32)
        middle = (delta - high).astype(BF16).astype(F32)
        low = delta - high - middle
        parts = jnp.where(lane == 0, -high, jnp.where(lane == 1, -middle, -low))
        dox_ref[at, :hd] = do
        dox_ref[at, hd:] = jnp.where(lane < 3, parts, 0.0).astype(BF16)

    def slope(g, carry):
        at = pl.ds(pl.multiple_of(g * group, group), group)
        dp = transposed(dox_ref[at, :], vx_ref[...])
        ds_ref[at, :] = (e_ref[at, :] * dp).astype(BF16)
        return carry

    lax.fori_loop(0, heads * tok // group, slope, 0)
    for h in range(heads):
        at, cols = slice(h * tok, (h + 1) * tok), slice(h * hd, (h + 1) * hd)
        dq = jnp.dot(ds_ref[at, :], kx_ref[:, :hd], preferred_element_type=F32)
        dq_ref[:, cols] = (dq * scale).astype(BF16)
    q_t = qx_ref[:, :hd].T
    do_t = dox_ref[:, :hd].T
    wide = 4

    def one_peer(c, carry):
        cols = pl.ds(pl.multiple_of(c * wide * tok, wide * tok), wide * tok)
        dk = jnp.dot(q_t, ds_ref[:, cols], preferred_element_type=F32) * scale
        dv = jnp.dot(do_t, p_ref[:, cols], preferred_element_type=F32)
        for i in range(wide):
            dkv_ref[c * wide + i, :hd, :] = dk[:, i * tok : (i + 1) * tok].astype(BF16)
            dkv_ref[c * wide + i, hd:, :] = dv[:, i * tok : (i + 1) * tok].astype(BF16)
        return carry

    lax.fori_loop(0, peers // wide, one_peer, 0)
    dnkv_ref[:hd, :] = jnp.dot(q_t, ds_ref[:, peers * tok :], preferred_element_type=F32) * scale
    dnkv_ref[hd:, :] = jnp.dot(do_t, p_ref[:, peers * tok :], preferred_element_type=F32)


def row_grad_kernel(recv_ref, dnkv_ref, cpre_ref, npre_ref, gain_ref, g_ref):
    rows, hd = cpre_ref.shape
    summed = recv_ref[0].astype(F32)
    for c in range(1, recv_ref.shape[0]):
        summed = summed + recv_ref[c].astype(F32)
    for copy, (grad_t, pre_ref) in enumerate(((summed, cpre_ref), (dnkv_ref[...], npre_ref))):
        at = slice(copy * rows, (copy + 1) * rows)
        pre = pre_ref[...]
        inverse = lax.rsqrt(jnp.mean(pre * pre, axis=1, keepdims=True) + EPSILON)
        scaled = grad_t[:hd].T * gain_ref[...]
        inner = jnp.mean(scaled * pre, axis=1, keepdims=True)
        pre_grad = inverse * scaled - pre * inverse * inverse * inverse * inner
        g_ref[at, :hd] = pre_grad.astype(BF16)
        g_ref[at, hd:] = grad_t[hd:].T.astype(BF16)


def weight_kernel(mine_ref, theirs_ref, g_ref, their_g_ref, dw_ref):
    dw_ref[...] = (
        jnp.dot(mine_ref[...], g_ref[...], preferred_element_type=F32)
        + jnp.dot(theirs_ref[...], their_g_ref[...], preferred_element_type=F32)
    ).astype(BF16)


def whole(*shape):
    return pl.BlockSpec(shape, lambda *_: (0,) * len(shape))


def limit(mib):
    return pltpu.CompilerParams(vmem_limit_bytes=mib * MIB)


def per_device(
    clean_hidden, noisy_hidden, noisy_query, out_grad, kv_weight, key_gain,
    doc_lengths, clean_place, noisy_place,
):
    rows, width = clean_hidden.shape[1:]
    hd = key_gain.shape[0]
    cp = ("y", "x")
    peers, zs = lax.axis_size(cp), lax.axis_size("z")
    total = clean_place.shape[1] * BLK + rows
    heads = noisy_query.shape[2] // hd
    clean, noisy = clean_hidden[0], noisy_hidden[0]
    gain = key_gain.reshape(1, hd)
    cp_index = lax.axis_index(cp).reshape(1, 1).astype(jnp.int32)
    core_index = lax.axis_index("core").reshape(1, 1).astype(jnp.int32)
    smem = pl.BlockSpec(memory_space=pltpu.SMEM)
    shape = jax.ShapeDtypeStruct
    swap = [(0, 1), (1, 0)]

    steps = 5
    part = width // steps
    spread, clean_pre = pl.pallas_call(
        clean_kernel,
        grid=(steps,),
        in_specs=[
            pl.BlockSpec((rows, part), lambda s: (0, s)),
            pl.BlockSpec((part, 2 * hd), lambda s: (s, 0)),
            whole(1, hd),
        ],
        out_specs=[whole(peers, rows, 2 * hd), whole(rows, hd)],
        out_shape=[shape((peers, rows, 2 * hd), BF16), shape((rows, hd), F32)],
        scratch_shapes=[pltpu.VMEM((rows, 2 * hd), F32)],
        compiler_params=limit(10),
        cost_estimate=pl.CostEstimate(
            flops=4 * rows * width * hd, bytes_accessed=5 * MIB, transcendentals=0
        ),
        name="clean",
    )(clean, kv_weight, gain)

    spread, clean_later, noisy_later = lax.optimization_barrier((spread, clean, noisy))
    gathered = lax.all_to_all(spread, cp, 0, 0, tiled=True)

    slab = width // zs
    per = slab // (2 * peers)
    turned = shape((peers, per, zs, 2 * rows), BF16)
    nkv, noisy_pre, mask, mine, other = pl.pallas_call(
        prepare_kernel,
        grid=(zs,),
        in_specs=[smem] * 5
        + [pl.BlockSpec((rows, slab), lambda s: (0, s))] * 2
        + [pl.BlockSpec((slab, 2 * hd), lambda s: (s, 0)), whole(1, hd)],
        out_specs=[
            whole(rows, 2 * hd),
            whole(rows, hd),
            whole(total, hd),
            whole(*turned.shape),
            whole(*turned.shape),
        ],
        out_shape=[
            shape((rows, 2 * hd), BF16),
            shape((rows, hd), F32),
            shape((total, hd), BF16),
            turned,
            turned,
        ],
        scratch_shapes=[
            pltpu.VMEM((rows, 2 * hd), F32),
            pltpu.VMEM((2, 2, width // 2, 128), F32),
        ],
        compiler_params=limit(24),
        cost_estimate=pl.CostEstimate(
            flops=4 * rows * width * hd, bytes_accessed=12 * MIB, transcendentals=0
        ),
        name="prepare",
    )(
        cp_index, core_index, doc_lengths, clean_place, noisy_place,
        clean_later, noisy_later, kv_weight, gain,
    )
    theirs = lax.ppermute(other, "core", swap)

    attention, query_grad, dkv, dnkv = pl.pallas_call(
        attention_kernel,
        out_shape=[
            shape((rows, heads * hd), BF16),
            shape((rows, heads * hd), BF16),
            shape((peers, 2 * hd, rows), BF16),
            shape((2 * hd, rows), F32),
        ],
        scratch_shapes=[
            pltpu.VMEM((total, 2 * hd), BF16),
            pltpu.VMEM((total, 2 * hd), BF16),
            pltpu.VMEM((heads * rows, 2 * hd), BF16),
            pltpu.VMEM((heads * rows, 2 * hd), BF16),
            pltpu.VMEM((heads * rows, total), F32),
            pltpu.VMEM((heads * rows, total), BF16),
            pltpu.VMEM((heads * rows, total), BF16),
        ],
        compiler_params=limit(44),
        cost_estimate=pl.CostEstimate(
            flops=12 * heads * rows * total * hd,
            bytes_accessed=4 * MIB,
            transcendentals=heads * rows * total,
        ),
        name="attend",
    )(noisy_query[0], out_grad[0], gathered, nkv, mask)

    received = lax.all_to_all(dkv, cp, 0, 0, tiled=True)

    row_grad = pl.pallas_call(
        row_grad_kernel,
        out_shape=shape((2 * rows, 2 * hd), BF16),
        compiler_params=limit(8),
        name="row_grad",
    )(received, dnkv, clean_pre, noisy_pre, gain)
    their_grad = lax.ppermute(row_grad, "core", swap)

    columns = width // 2
    tile = columns // 4
    flat = (columns, 2 * rows)
    both = pl.pallas_call(
        weight_kernel,
        grid=(columns // tile,),
        in_specs=[pl.BlockSpec((tile, 2 * rows), lambda s: (s, 0))] * 2
        + [whole(2 * rows, 2 * hd)] * 2,
        out_specs=pl.BlockSpec((tile, 2 * hd), lambda s: (s, 0)),
        out_shape=shape((columns, 2 * hd), BF16),
        compiler_params=limit(8),
        name="weight",
    )(mine.reshape(flat), theirs.reshape(flat), row_grad, their_grad)

    both = lax.all_to_all(both.reshape(peers, per, zs, 2 * hd), cp, 0, 0, tiled=True)
    term = jnp.sum(both.astype(F32), axis=0).astype(BF16)
    term = lax.all_to_all(jnp.swapaxes(term, 0, 1), "z", 0, 0, tiled=True)
    share = jnp.sum(term.astype(F32), axis=0).astype(BF16)
    return (attention[None], query_grad[None], share)


def solution(mesh):
    zs, cps = mesh.devices.shape[0] // 2, mesh.devices.shape[1]
    side = int(round(cps**0.5))
    grid = Mesh(mesh.devices.reshape(zs, 2, cps // side, side), ("z", "core", "y", "x"))
    grp, cp = ("z", "core"), ("y", "x")
    in_specs = (
        P(grp, cp, None),
        P(grp, cp, None),
        P(grp, cp, None),
        P(grp, cp, None),
        P(),
        P(),
        P(grp, None),
        P(grp, None),
        P(grp, None),
    )
    out_specs = (P(grp, cp, None), P(grp, cp, None), P(grp + cp, None))
    return jax.shard_map(
        per_device, mesh=grid, in_specs=in_specs, out_specs=out_specs, check_vma=False
    )
```

time: 128 us -> 109 us (0.85)
  waiting for transfers between devices: 18.5 us -> 4.85 us
  Pallas kernels: 35.9 us -> 24 us
  local copies, waits for them, and re-layouts: 1 us -> 10.3 us
  blocking collectives: 63.5 us -> 60.3 us
  starting transfers between devices: 4.9 us -> 7.72 us
  other arithmetic: 2.53 us -> 0.8 us
    pallas_call x3 -> x5, Pallas kernels: 35.9 us -> 24 us  [the longest x1 12 us: per_device(): pl.pallas_call(attention_kernel, out_shape=[shape((rows, heads * hd), BF1...]
    all_to_all x1, waiting for transfers between devices: 15.2 us -> 3.52 us  [per_device(): gathered = lax.all_to_all(spread, cp, 0, 0, tiled=True)]
    unnamed x2 -> x30, local copies, waits for them, and re-layouts: 0.98 us -> 10.3 us
    all_to_all x2, blocking collectives: 46.5 us -> 43.3 us  [the longest x1 23.2 us: per_device(): lax.all_to_all(both.reshape(peers, per, zs, 2 * hd), cp, 0, 0, tiled=True)]
    all_to_all x1, starting transfers between devices: 4.9 us -> 7.62 us  [per_device(): gathered = lax.all_to_all(spread, cp, 0, 0, tiled=True)]
    ppermute x1 -> x2, waiting for transfers between devices: 3.24 us -> 1.33 us  [the longest x1 1.32 us: per_device(): their_grad = lax.ppermute(row_grad, 'core', swap)]
    convert_element_type x1 -> x0, other arithmetic: 1.73 us -> none  [per_device(): both = (keep.astype(F32) + other.astype(F32)).astype(BF16)]
  transfers between devices with their start and end apart: 2 -> 3, of which waited for: 2 -> 2; matrix products, arithmetic and copies ran while one was open for 0% -> 0% of each run, Pallas kernels for 0% -> 19%
where the time goes in v2:
time: 109 us
  blocking collectives  60.3 us (55%)
  Pallas kernels  24 us (22%)
  local copies, waits for them, and re-layouts  10.3 us (9%)
  starting transfers between devices  7.72 us (7%)
  waiting for transfers between devices  4.85 us (4%)
    all_to_all x1, blocking collectives, per_device(): lax.all_to_all(both.reshape(peers, per, zs, 2 * hd), cp, 0, 0, tiled=True)  23.2 us
    all_to_all x1, blocking collectives, per_device(): received = lax.all_to_all(dkv, cp, 0, 0, tiled=True)  20.1 us
    all_to_all x1, blocking collectives, per_device(): term = lax.all_to_all(jnp.swapaxes(term, 0, 1), 'z', 0, 0, tiled=True)  17 us
    pallas_call x1, Pallas kernels, per_device(): pl.pallas_call(attention_kernel, out_shape=[shape((rows, heads * hd), BF1...  12 us
    unnamed x30, local copies, waits for them, and re-layouts  10.3 us
    pallas_call x1, Pallas kernels, per_device(): pl.pallas_call(prepare_kernel, grid=(zs,), in_specs=[smem] * 5 + [pl.Bloc...  8.61 us
    all_to_all x1, starting transfers between devices, per_device(): gathered = lax.all_to_all(spread, cp, 0, 0, tiled=True)  7.62 us
    all_to_all x1, waiting for transfers between devices, per_device(): gathered = lax.all_to_all(spread, cp, 0, 0, tiled=True)  3.52 us
  transfers between devices with their start and end apart: 3, of which 2 were waited for; matrix products, arithmetic and copies ran while one was open for 0% of the time, Pallas kernels for 19%

profile of v2, /device:TPU:2, one launch (start us, length us, event | category | flops | bytes accessed | tf_op | source)
XLA Modules:
  0.0 108.7 jit_solution(3352969805818268526)
XLA Ops:
  0.6 0.0 copy-start
  0.6 1.7 %copy-done = bf16[5120,256]{1,0:T(8,128)(2,1)S(1)} copy-done((bf16[5120,256]{1,0:T(8,128)(2,1)S(1)}, bf16[5120,256]{1,0:T(8,128)(2,1)}, u32[]{:S(2)}) %copy-start) | copy-done | bytes 2621464
  2.4 0.0 copy-start.2
  2.4 1.3 %copy-done.2 = bf16[1,128,5120]{2,1,0:T(8,128)(2,1)S(1)} copy-done((bf16[1,128,5120]{2,1,0:T(8,128)(2,1)S(1)}, bf16[1,128,5120]{2,1,0:T(8,128)(2,1)}, u32[]{:S(2)}) %copy-start.2) | copy-done | bytes 1310744
  3.7 0.0 copy-start.8
  3.7 0.7 copy-done.8
  4.3 0.0 copy-start.1
  4.3 1.6 %clean.1 = (bf16[16,128,256]{2,1,0:T(8,128)(2,1)S(1)}, f32[128,128]{1,0:T(8,128)S(1)}) custom-call(bf16[128,5120]{1,0:T(8,128)(2,1)S(1)} %bitcast.14, bf16[5120,256]{1,0:T(8,128)(2,1)S(1)} %copy-done, f32[1,128]{1,0:T(1,128)S(1)} %bitcast.19), custom_call_target="tpu_custom_call" | custom-call | flops 335544320 | bytes 5242880 | tf_op jit(solution)/shard_map/clean/pallas_call | solution.py:250
  6.0 0.0 copy-start.7
  6.0 1.0 copy-done.7
  6.9 0.0 copy-start.9
  6.9 0.0 copy-start.10
  6.9 0.0 copy-start.11
  6.9 0.0 copy-start.12
  6.9 7.6 %all-to-all-start = ((bf16[16,128,256]{2,1,0:T(8,128)(2,1)}), bf16[16,128,256]{2,1,0:T(8,128)(2,1)}, u32[]{:S(2)}, u32[]{:S(2)}) async-start(bf16[16,128,256]{2,1,0:T(8,128)(2,1)} %copy-done.7), calls=%async_computation | async-start | bytes 2097152 | tf_op jit(solution)/shard_map/all_to_all | solution.py:269
  14.6 0.0 copy-done.1
  14.6 0.0 copy-done.9
  14.6 0.0 copy-done.10
  14.6 0.0 copy-done.11
  14.6 0.0 copy-done.12
  14.6 0.0 copy-start.3
  14.6 1.3 %copy-done.3 = bf16[1,128,5120]{2,1,0:T(8,128)(2,1)S(1)} copy-done((bf16[1,128,5120]{2,1,0:T(8,128)(2,1)S(1)}, bf16[1,128,5120]{2,1,0:T(8,128)(2,1)}, u32[]{:S(2)}) %copy-start.3) | copy-done | bytes 1310744
  15.9 0.0 copy-start.6
  15.9 1.3 %copy-done.6 = bf16[1,128,5120]{2,1,0:T(8,128)(2,1)S(1)} copy-done((bf16[1,128,5120]{2,1,0:T(8,128)(2,1)S(1)}, bf16[1,128,5120]{2,1,0:T(8,128)(2,1)}, u32[]{:S(2)}) %copy-start.6) | copy-done | bytes 1310744
  17.2 8.6 %prepare.1 = (bf16[128,256]{1,0:T(8,128)(2,1)S(1)}, f32[128,128]{1,0:T(8,128)S(1)}, bf16[2176,128]{1,0:T(8,128)(2,1)S(1)}, bf16[16,20,8,256]{3,2,1,0:T(8,128)(2,1)S(1)}, bf16[16,20,8,256]{3,2,1,0:T(8,128)(2,1)}) custom-call(s32[1,1]{1,0:T(1,128)} %bitcast.5.cp_ref, s32[1,1]{1,0:T(1,128)} %bitcast.6.core_ref, s32[1,4]{1,0:T(1,128)S(1)} %copy-done.10, ...), custom_call_target="tpu_custom_call" | custom-call | flops 335544320 | bytes 12582912 | tf_op jit(solution)/shard_map/prepare/pallas_call | solution.py:274
  25.9 0.0 copy-start.4
  25.9 1.1 copy-done.4
  26.9 0.0 collective-permute-start
  26.9 3.5 %all-to-all-done.ckv_ref = bf16[16,128,256]{2,1,0:T(8,128)(2,1)} async-done(((bf16[16,128,256]{2,1,0:T(8,128)(2,1)}), bf16[16,128,256]{2,1,0:T(8,128)(2,1)}, u32[]{:S(2)}, u32[]{:S(2)}) %all-to-all-start) | async-done | bytes 1048608 | tf_op jit(solution)/shard_map/all_to_all | solution.py:269
  30.5 0.0 copy-start.13
  30.5 0.9 copy-done.13
  31.4 0.0 copy-start.14
  31.4 0.9 copy-done.14
  32.4 12.0 %attend.1 = (bf16[128,1024]{1,0:T(8,128)(2,1)}, bf16[128,1024]{1,0:T(8,128)(2,1)}, bf16[16,256,128]{2,1,0:T(8,128)(2,1)S(1)}, f32[256,128]{1,0:T(8,128)S(1)}) custom-call(bf16[128,1024]{1,0:T(8,128)(2,1)S(1)} %bitcast.22, bf16[128,1024]{1,0:T(8,128)(2,1)S(1)} %bitcast.23, bf16[16,128,256]{2,1,0:T(8,128)(2,1)} %all-to-all-done.ckv_ref, ...), custom_call_target="tpu_custom_call" | custom-call | flops 3422552064 | bytes 4194304 | tf_op jit(solution)/shard_map/attend/pallas_call | solution.py:309
  44.4 0.0 copy-start.5
  44.4 20.1 %all_to_all.20.recv_ref = bf16[16,256,128]{2,1,0:T(8,128)(2,1)S(1)} all-to-all(bf16[16,256,128]{2,1,0:T(8,128)(2,1)S(1)} %get-tuple-element.27), channel_id=1, replica_groups=mesh['z'=8,'core'=2,'y'=4,'x'=4] {'y','x'}, dimensions={0} | all-to-all | bytes 2097152 | tf_op jit(solution)/shard_map/all_to_all | solution.py:335
  64.5 0.4 row_grad.1.g_ref
  64.9 0.1 collective-permute-start.1
  65.0 0.0 collective-permute-done
  65.0 1.3 %collective-permute-done.1.their_g_ref = bf16[256,256]{1,0:T(8,128)(2,1)S(1)} collective-permute-done((bf16[256,256]{1,0:T(8,128)(2,1)S(1)}, bf16[256,256]{1,0:T(8,128)(2,1)S(1)}, u32[]{:S(2)}, u32[]{:S(2)}) %collective-permute-start.1) | collective-permute-done | bytes 131104 | tf_op jit(solution)/shard_map/ppermute | solution.py:343
  66.3 0.0 copy-done.5
  66.3 1.3 %weight.1 = bf16[2560,256]{1,0:T(8,128)(2,1)S(1)} custom-call(bf16[2560,256]{1,0:T(8,128)(2,1)S(1)} %bitcast.16, bf16[2560,256]{1,0:T(8,128)(2,1)S(1)} %bitcast.17, bf16[256,256]{1,0:T(8,128)(2,1)S(1)} %row_grad.1.g_ref, bf16[256,256]{1,0:T(8,128)(2,1)S(1)} %collective-permute-done.1.their_g_ref), custom_call_target="tpu_custom_call" | custom-call | tf_op jit(solution)/shard_map/weight/pallas_call | solution.py:348
  67.7 23.2 %all_to_all.21 = bf16[16,20,8,256]{3,2,1,0:T(8,128)(2,1)S(1)} all-to-all(bf16[16,20,8,256]{3,2,1,0:T(8,128)(2,1)S(1)} %bitcast.13), channel_id=1, replica_groups=mesh['z'=8,'core'=2,'y'=4,'x'=4] {'y','x'}, dimensions={0} | all-to-all | bytes 2621440 | tf_op jit(solution)/shard_map/all_to_all | solution.py:359
  90.9 0.2 reduce_sum.24
  91.1 17.0 %all_to_all.22 = bf16[8,20,256]{2,1,0:T(8,128)(2,1)S(1)} all-to-all(bf16[8,20,256]{2,1,0:T(8,128)(2,1)S(1)} %copy.12), channel_id=1, replica_groups=mesh['z'=8,'core'=2,'y'=4,'x'=4] {'z'}, dimensions={0} | all-to-all | bytes 163840 | tf_op jit(solution)/shard_map/all_to_all | solution.py:361
  108.1 0.6 reduce_sum.25
  (1 shorter events, 0.0 us)
Async XLA Ops:
  0.6 1.7 %copy-start = (bf16[5120,256]{1,0:T(8,128)(2,1)S(1)}, bf16[5120,256]{1,0:T(8,128)(2,1)}, u32[]{:S(2)}) copy-start(bf16[5120,256]{1,0:T(8,128)(2,1)} %w_ref.3) | copy-start | bytes 7864324
  2.4 1.3 %copy-start.2 = (bf16[1,128,5120]{2,1,0:T(8,128)(2,1)S(1)}, bf16[1,128,5120]{2,1,0:T(8,128)(2,1)}, u32[]{:S(2)}) copy-start(bf16[1,128,5120]{2,1,0:T(8,128)(2,1)} %param.9) | copy-start | bytes 3932164
  3.7 0.7 copy-start.8
  4.3 10.2 %copy-start.1 = (bf16[5120,256]{1,0:T(8,128)(2,1)S(1)}, bf16[5120,256]{1,0:T(8,128)(2,1)}, u32[]{:S(2)}) copy-start(bf16[5120,256]{1,0:T(8,128)(2,1)} %w_ref.3) | copy-start | bytes 7864324
  6.0 1.0 copy-start.7
  6.9 7.6 %copy-start.9 = (f32[128]{0:T(128)S(1)}, f32[128]{0:T(128)}, u32[]{:S(2)}) copy-start(f32[128]{0:T(128)} %param.14) | copy-start | bytes 1540
  6.9 7.6 %copy-start.10 = (s32[1,4]{1,0:T(1,128)S(1)}, s32[1,4]{1,0:T(1,128)}, u32[]{:S(2)}) copy-start(s32[1,4]{1,0:T(1,128)} %len_ref.1) | copy-start | bytes 52
  6.9 7.7 %copy-start.11 = (s32[1,32]{1,0:T(1,128)S(1)}, s32[1,32]{1,0:T(1,128)}, u32[]{:S(2)}) copy-start(s32[1,32]{1,0:T(1,128)} %cplace_ref.1) | copy-start | bytes 388
  6.9 7.7 %copy-start.12 = (s32[1,32]{1,0:T(1,128)S(1)}, s32[1,32]{1,0:T(1,128)}, u32[]{:S(2)}) copy-start(s32[1,32]{1,0:T(1,128)} %nplace_ref.1) | copy-start | bytes 388
  6.9 23.5 %all-to-all-start = ((bf16[16,128,256]{2,1,0:T(8,128)(2,1)}), bf16[16,128,256]{2,1,0:T(8,128)(2,1)}, u32[]{:S(2)}, u32[]{:S(2)}) async-start(bf16[16,128,256]{2,1,0:T(8,128)(2,1)} %copy-done.7), calls=%async_computation | async-start | bytes 2097152 | tf_op jit(solution)/shard_map/all_to_all | solution.py:269
  14.6 1.3 %copy-start.3 = (bf16[1,128,5120]{2,1,0:T(8,128)(2,1)S(1)}, bf16[1,128,5120]{2,1,0:T(8,128)(2,1)}, u32[]{:S(2)}) copy-start(bf16[1,128,5120]{2,1,0:T(8,128)(2,1)} %param.9) | copy-start | bytes 3932164
  15.9 1.3 %copy-start.6 = (bf16[1,128,5120]{2,1,0:T(8,128)(2,1)S(1)}, bf16[1,128,5120]{2,1,0:T(8,128)(2,1)}, u32[]{:S(2)}) copy-start(bf16[1,128,5120]{2,1,0:T(8,128)(2,1)} %param.10) | copy-start | bytes 3932164
  25.9 1.1 copy-start.4
  26.9 38.1 %collective-permute-start = (bf16[16,20,8,256]{3,2,1,0:T(8,128)(2,1)}, bf16[16,20,8,256]{3,2,1,0:T(8,128)(2,1)S(1)}, u32[]{:S(2)}, u32[]{:S(2)}) collective-permute-start(bf16[16,20,8,256]{3,2,1,0:T(8,128)(2,1)} %get-tuple-element.26), channel_id=1, source_target_pairs={{0,16},{16,0},{1,17},{17,1},{2,18},{18,2},{3,19},{19,3},{4,20},{20... | collective-permute-start | bytes 3932168 | tf_op jit(solution)/shard_map/ppermute | solution.py:307
  30.5 1.0 copy-start.13
  31.4 0.9 copy-start.14
  44.4 22.0 %copy-start.5 = (bf16[16,20,8,256]{3,2,1,0:T(8,128)(2,1)S(1)}, bf16[16,20,8,256]{3,2,1,0:T(8,128)(2,1)}, u32[]{:S(2)}) copy-start(bf16[16,20,8,256]{3,2,1,0:T(8,128)(2,1)} %copy-done.4) | copy-start | bytes 3932164
  64.9 1.4 %collective-permute-start.1 = (bf16[256,256]{1,0:T(8,128)(2,1)S(1)}, bf16[256,256]{1,0:T(8,128)(2,1)S(1)}, u32[]{:S(2)}, u32[]{:S(2)}) collective-permute-start(bf16[256,256]{1,0:T(8,128)(2,1)S(1)} %row_grad.1.g_ref), channel_id=1, source_target_pairs={{0,16},{16,0},{1,17},{17,1},{2,18},{18,2},{3,19},{19,3},{4,20},{20... | collective-permute-start | bytes 393224 | tf_op jit(solution)/shard_map/ppermute | solution.py:343

commit v3 on v2

--- a/solution.py
+++ b/solution.py
@@ -35,17 +35,42 @@
         acc_ref[...] += part
 
 
-def clean_kernel(clean_ref, w_ref, gain_ref, spread_ref, pre_ref, acc_ref):
+def clean_kernel(
+    clean_ref, w_ref, gain_ref, spread_ref, pre_ref,
+    rows_ref, weight_ref, kv_ref, rows_sem, weight_sem, out_sem,
+):
     hd = gain_ref.shape[1]
-    accumulate(acc_ref, jnp.dot(clean_ref[...], w_ref[...], preferred_element_type=F32))
-
-    @pl.when(pl.program_id(0) == pl.num_programs(0) - 1)
-    def _():
-        pre, keys, values = keys_values(acc_ref[...], gain_ref[...])
-        pre_ref[...] = pre
-        for dest in range(spread_ref.shape[0]):
-            spread_ref[dest, :, :hd] = keys
-            spread_ref[dest, :, hd:] = values
+    parts = rows_ref.shape[0]
+    part = rows_ref.shape[2]
+    loads = []
+    for i in range(parts):
+        at = pl.ds(i * part, part)
+        loads.append(
+            (
+                pltpu.make_async_copy(w_ref.at[at, :], weight_ref.at[i], weight_sem.at[i]),
+                pltpu.make_async_copy(clean_ref.at[:, at], rows_ref.at[i], rows_sem.at[i]),
+            )
+        )
+        for load in loads[i]:
+            load.start()
+    joined = None
+    for i in range(parts):
+        for load in loads[i]:
+            load.wait()
+        term = jnp.dot(rows_ref[i], weight_ref[i], preferred_element_type=F32)
+        joined = term if joined is None else joined + term
+    pre, keys, values = keys_values(joined, gain_ref[...])
+    pre_ref[...] = pre
+    kv_ref[:, :hd] = keys
+    kv_ref[:, hd:] = values
+    stores = [
+        pltpu.make_async_copy(kv_ref, spread_ref.at[dest], out_sem.at[dest])
+        for dest in range(spread_ref.shape[0])
+    ]
+    for store in stores:
+        store.start()
+    for store in stores:
+        store.wait()
 
 
 def prepare_kernel(
@@ -151,7 +176,7 @@
         p_ref[at, :] = e.astype(BF16)
         return carry
 
-    lax.fori_loop(0, heads * tok // group, weigh, 0)
+    lax.fori_loop(0, heads * tok // group, weigh, 0, unroll=True)
     for h in range(heads):
         at, cols = slice(h * tok, (h + 1) * tok), slice(h * hd, (h + 1) * hd)
         o = jnp.dot(p_ref[at, :], vx_ref[...], preferred_element_type=F32)
@@ -173,7 +198,7 @@
         ds_ref[at, :] = (e_ref[at, :] * dp).astype(BF16)
         return carry
 
-    lax.fori_loop(0, heads * tok // group, slope, 0)
+    lax.fori_loop(0, heads * tok // group, slope, 0, unroll=True)
     for h in range(heads):
         at, cols = slice(h * tok, (h + 1) * tok), slice(h * hd, (h + 1) * hd)
         dq = jnp.dot(ds_ref[at, :], kx_ref[:, :hd], preferred_element_type=F32)
@@ -191,7 +216,7 @@
             dkv_ref[c * wide + i, hd:, :] = dv[:, i * tok : (i + 1) * tok].astype(BF16)
         return carry
 
-    lax.fori_loop(0, peers // wide, one_peer, 0)
+    lax.fori_loop(0, peers // wide, one_peer, 0, unroll=True)
     dnkv_ref[:hd, :] = jnp.dot(q_t, ds_ref[:, peers * tok :], preferred_element_type=F32) * scale
     dnkv_ref[hd:, :] = jnp.dot(do_t, p_ref[:, peers * tok :], preferred_element_type=F32)
 
@@ -245,20 +270,23 @@
     shape = jax.ShapeDtypeStruct
     swap = [(0, 1), (1, 0)]
 
-    steps = 5
-    part = width // steps
+    parts = 5
+    part = width // parts
+    anywhere = pl.BlockSpec(memory_space=pl.ANY)
     spread, clean_pre = pl.pallas_call(
         clean_kernel,
-        grid=(steps,),
-        in_specs=[
-            pl.BlockSpec((rows, part), lambda s: (0, s)),
-            pl.BlockSpec((part, 2 * hd), lambda s: (s, 0)),
-            whole(1, hd),
-        ],
-        out_specs=[whole(peers, rows, 2 * hd), whole(rows, hd)],
+        in_specs=[anywhere, anywhere, pl.BlockSpec(memory_space=pltpu.VMEM)],
+        out_specs=[anywhere, pl.BlockSpec(memory_space=pltpu.VMEM)],
         out_shape=[shape((peers, rows, 2 * hd), BF16), shape((rows, hd), F32)],
-        scratch_shapes=[pltpu.VMEM((rows, 2 * hd), F32)],
-        compiler_params=limit(10),
+        scratch_shapes=[
+            pltpu.VMEM((parts, rows, part), BF16),
+            pltpu.VMEM((parts, part, 2 * hd), BF16),
+            pltpu.VMEM((rows, 2 * hd), BF16),
+            pltpu.SemaphoreType.DMA((parts,)),
+            pltpu.SemaphoreType.DMA((parts,)),
+            pltpu.SemaphoreType.DMA((peers,)),
+        ],
+        compiler_params=limit(60),
         cost_estimate=pl.CostEstimate(
             flops=4 * rows * width * hd, bytes_accessed=5 * MIB, transcendentals=0
         ),
@@ -295,7 +323,7 @@
             pltpu.VMEM((rows, 2 * hd), F32),
             pltpu.VMEM((2, 2, width // 2, 128), F32),
         ],
-        compiler_params=limit(24),
+        compiler_params=limit(63),
         cost_estimate=pl.CostEstimate(
             flops=4 * rows * width * hd, bytes_accessed=12 * MIB, transcendentals=0
         ),
@@ -323,7 +351,7 @@
             pltpu.VMEM((heads * rows, total), BF16),
             pltpu.VMEM((heads * rows, total), BF16),
         ],
-        compiler_params=limit(44),
+        compiler_params=limit(60),
         cost_estimate=pl.CostEstimate(
             flops=12 * heads * rows * total * hd,
             bytes_accessed=4 * MIB,

time: 109 us -> 104 us (0.954)
  local copies, waits for them, and re-layouts: 10.3 us -> 0.04 us
  Pallas kernels: 24 us -> 28 us
    unnamed x30 -> x10, local copies, waits for them, and re-layouts: 10.3 us -> 0.02 us
    pallas_call x1, Pallas kernels: 1.61 us -> 4.92 us  [per_device(): pl.pallas_call(clean_kernel, in_specs=[anywhere, anywhere, pl.BlockSpec(m...]
    pallas_call x1, Pallas kernels: 8.61 us -> 11.8 us  [per_device(): pl.pallas_call(prepare_kernel, grid=(zs,), in_specs=[smem] * 5 + [pl.Bloc...]
    pallas_call x1, Pallas kernels: 12 us -> 9.53 us  [per_device(): pl.pallas_call(attention_kernel, out_shape=[shape((rows, heads * hd), BF1...]
  transfers between devices with their start and end apart: 3 -> 3, of which waited for: 2 -> 2; matrix products, arithmetic and copies ran while one was open for 0% -> 0% of each run, Pallas kernels for 19% -> 21%
where the time goes in v3:
time: 104 us; the launch traced here: 103 us
  blocking collectives  60.6 us (58%)
  Pallas kernels  28 us (27%)
  starting transfers between devices  7.58 us (7%)
  waiting for transfers between devices  5.44 us (5%)
    all_to_all x1, blocking collectives, per_device(): lax.all_to_all(both.reshape(peers, per, zs, 2 * hd), cp, 0, 0, tiled=True)  23.3 us
    all_to_all x1, blocking collectives, per_device(): received = lax.all_to_all(dkv, cp, 0, 0, tiled=True)  20.4 us
    all_to_all x1, blocking collectives, per_device(): term = lax.all_to_all(jnp.swapaxes(term, 0, 1), 'z', 0, 0, tiled=True)  17 us
    pallas_call x1, Pallas kernels, per_device(): pl.pallas_call(prepare_kernel, grid=(zs,), in_specs=[smem] * 5 + [pl.Bloc...  11.8 us
    pallas_call x1, Pallas kernels, per_device(): pl.pallas_call(attention_kernel, out_shape=[shape((rows, heads * hd), BF1...  9.53 us
    all_to_all x1, starting transfers between devices, per_device(): gathered = lax.all_to_all(spread, cp, 0, 0, tiled=True)  7.49 us
    pallas_call x1, Pallas kernels, per_device(): pl.pallas_call(clean_kernel, in_specs=[anywhere, anywhere, pl.BlockSpec(m...  4.92 us
    all_to_all x1, waiting for transfers between devices, per_device(): gathered = lax.all_to_all(spread, cp, 0, 0, tiled=True)  4.11 us
  transfers between devices with their start and end apart: 3, of which 2 were waited for; matrix products, arithmetic and copies ran while one was open for 0% of the time, Pallas kernels for 21%

profile of v3, /device:TPU:2, one launch (start us, length us, event | category | flops | bytes accessed | tf_op | source)
XLA Modules:
  0.0 103.2 jit_solution(12565213567986628001)
XLA Ops:
  0.6 4.9 %clean.1 = (bf16[16,128,256]{2,1,0:T(8,128)(2,1)}, f32[128,128]{1,0:T(8,128)}) custom-call(bf16[128,5120]{1,0:T(8,128)(2,1)} %bitcast.19, bf16[5120,256]{1,0:T(8,128)(2,1)} %w_ref.3, f32[1,128]{1,0:T(1,128)} %bitcast.16), custom_call_target="tpu_custom_call" | custom-call | flops 335544320 | bytes 5242880 | tf_op jit(solution)/shard_map/clean/pallas_call | solution.py:276
  5.6 7.5 %all-to-all-start = ((bf16[16,128,256]{2,1,0:T(8,128)(2,1)}), bf16[16,128,256]{2,1,0:T(8,128)(2,1)}, u32[]{:S(2)}, u32[]{:S(2)}) async-start(bf16[16,128,256]{2,1,0:T(8,128)(2,1)} %get-tuple-element.18), calls=%async_computation | async-start | bytes 2097152 | tf_op jit(solution)/shard_map/all_to_all | solution.py:297
  13.0 11.8 %prepare.1 = (bf16[128,256]{1,0:T(8,128)(2,1)}, f32[128,128]{1,0:T(8,128)}, bf16[2176,128]{1,0:T(8,128)(2,1)}, bf16[16,20,8,256]{3,2,1,0:T(8,128)(2,1)}, bf16[16,20,8,256]{3,2,1,0:T(8,128)(2,1)}) custom-call(s32[1,1]{1,0:T(1,128)} %bitcast.5.cp_ref, s32[1,1]{1,0:T(1,128)} %bitcast.6.core_ref, s32[1,4]{1,0:T(1,128)} %len_ref.1, s32[1,32]{1,0:T(1,128)} %cplace_ref.1, ...), custom_call_target="tpu_custom_call" | custom-call | flops 335544320 | bytes 12582912 | tf_op jit(solution)/shard_map/prepare/pallas_call | solution.py:302
  24.8 0.0 collective-permute-start
  24.8 4.1 %all-to-all-done.ckv_ref = bf16[16,128,256]{2,1,0:T(8,128)(2,1)} async-done(((bf16[16,128,256]{2,1,0:T(8,128)(2,1)}), bf16[16,128,256]{2,1,0:T(8,128)(2,1)}, u32[]{:S(2)}, u32[]{:S(2)}) %all-to-all-start) | async-done | bytes 1048608 | tf_op jit(solution)/shard_map/all_to_all | solution.py:297
  28.9 9.5 %attend.1 = (bf16[128,1024]{1,0:T(8,128)(2,1)}, bf16[128,1024]{1,0:T(8,128)(2,1)}, bf16[16,256,128]{2,1,0:T(8,128)(2,1)}, f32[256,128]{1,0:T(8,128)}) custom-call(bf16[128,1024]{1,0:T(8,128)(2,1)} %bitcast.23, bf16[128,1024]{1,0:T(8,128)(2,1)} %bitcast.24, bf16[16,128,256]{2,1,0:T(8,128)(2,1)} %all-to-all-done.ckv_ref, ...), custom_call_target="tpu_custom_call" | custom-call | flops 3422552064 | bytes 4194304 | tf_op jit(solution)/shard_map/attend/pallas_call | solution.py:337
  38.5 0.0 copy-start.1
  38.5 0.0 copy-start.2
  38.5 0.0 copy-start.3
  38.5 0.0 copy-start.4
  38.5 0.0 copy-start
  38.5 20.4 %all_to_all.20.recv_ref = bf16[16,256,128]{2,1,0:T(8,128)(2,1)S(1)} all-to-all(bf16[16,256,128]{2,1,0:T(8,128)(2,1)} %get-tuple-element.27), channel_id=1, replica_groups=mesh['z'=8,'core'=2,'y'=4,'x'=4] {'y','x'}, dimensions={0} | all-to-all | bytes 2097152 | tf_op jit(solution)/shard_map/all_to_all | solution.py:363
  58.9 0.0 copy-done.1
  58.9 0.0 copy-done.2
  58.9 0.0 copy-done.3
  58.9 0.0 copy-done.4
  58.9 0.4 row_grad.1.g_ref
  59.4 0.1 collective-permute-start.1
  59.5 0.0 collective-permute-done
  59.5 1.3 %collective-permute-done.1.their_g_ref = bf16[256,256]{1,0:T(8,128)(2,1)S(1)} collective-permute-done((bf16[256,256]{1,0:T(8,128)(2,1)S(1)}, bf16[256,256]{1,0:T(8,128)(2,1)S(1)}, u32[]{:S(2)}, u32[]{:S(2)}) %collective-permute-start.1) | collective-permute-done | bytes 131104 | tf_op jit(solution)/shard_map/ppermute | solution.py:371
  60.8 0.0 copy-done
  60.8 1.4 %weight.1 = bf16[2560,256]{1,0:T(8,128)(2,1)S(1)} custom-call(bf16[2560,256]{1,0:T(8,128)(2,1)S(1)} %bitcast.14, bf16[2560,256]{1,0:T(8,128)(2,1)S(1)} %bitcast.15, bf16[256,256]{1,0:T(8,128)(2,1)S(1)} %row_grad.1.g_ref, bf16[256,256]{1,0:T(8,128)(2,1)S(1)} %collective-permute-done.1.their_g_ref), custom_call_target="tpu_custom_call" | custom-call | tf_op jit(solution)/shard_map/weight/pallas_call | solution.py:376
  62.2 23.3 %all_to_all.21 = bf16[16,20,8,256]{3,2,1,0:T(8,128)(2,1)S(1)} all-to-all(bf16[16,20,8,256]{3,2,1,0:T(8,128)(2,1)S(1)} %bitcast.13), channel_id=1, replica_groups=mesh['z'=8,'core'=2,'y'=4,'x'=4] {'y','x'}, dimensions={0} | all-to-all | bytes 2621440 | tf_op jit(solution)/shard_map/all_to_all | solution.py:387
  85.4 0.2 reduce_sum.24
  85.6 17.0 %all_to_all.22 = bf16[8,20,256]{2,1,0:T(8,128)(2,1)S(1)} all-to-all(bf16[8,20,256]{2,1,0:T(8,128)(2,1)S(1)} %copy.12), channel_id=1, replica_groups=mesh['z'=8,'core'=2,'y'=4,'x'=4] {'z'}, dimensions={0} | all-to-all | bytes 163840 | tf_op jit(solution)/shard_map/all_to_all | solution.py:389
  102.6 0.6 reduce_sum.25
  (1 shorter events, 0.0 us)
Async XLA Ops:
  5.6 23.4 %all-to-all-start = ((bf16[16,128,256]{2,1,0:T(8,128)(2,1)}), bf16[16,128,256]{2,1,0:T(8,128)(2,1)}, u32[]{:S(2)}, u32[]{:S(2)}) async-start(bf16[16,128,256]{2,1,0:T(8,128)(2,1)} %get-tuple-element.18), calls=%async_computation | async-start | bytes 2097152 | tf_op jit(solution)/shard_map/all_to_all | solution.py:297
  24.8 34.6 %collective-permute-start = (bf16[16,20,8,256]{3,2,1,0:T(8,128)(2,1)}, bf16[16,20,8,256]{3,2,1,0:T(8,128)(2,1)S(1)}, u32[]{:S(2)}, u32[]{:S(2)}) collective-permute-start(bf16[16,20,8,256]{3,2,1,0:T(8,128)(2,1)} %get-tuple-element.26), channel_id=1, source_target_pairs={{0,16},{16,0},{1,17},{17,1},{2,18},{18,2},{3,19},{19,3},{4,20},{20... | collective-permute-start | bytes 3932168 | tf_op jit(solution)/shard_map/ppermute | solution.py:335
  38.5 20.5 %copy-start.1 = (f32[256,128]{1,0:T(8,128)S(1)}, f32[256,128]{1,0:T(8,128)}, u32[]{:S(2)}) copy-start(f32[256,128]{1,0:T(8,128)} %get-tuple-element.28.dnkv_ref) | copy-start | bytes 393220
  38.5 20.5 %copy-start.2 = (f32[128,128]{1,0:T(8,128)S(1)}, f32[128,128]{1,0:T(8,128)}, u32[]{:S(2)}) copy-start(f32[128,128]{1,0:T(8,128)} %get-tuple-element.29.cpre_ref) | copy-start | bytes 196612
  38.5 20.5 %copy-start.3 = (f32[128,128]{1,0:T(8,128)S(1)}, f32[128,128]{1,0:T(8,128)}, u32[]{:S(2)}) copy-start(f32[128,128]{1,0:T(8,128)} %get-tuple-element.30.npre_ref) | copy-start | bytes 196612
  38.5 20.5 %copy-start.4 = (f32[128]{0:T(128)S(1)}, f32[128]{0:T(128)}, u32[]{:S(2)}) copy-start(f32[128]{0:T(128)} %param.14) | copy-start | bytes 1540
  38.5 22.3 %copy-start = (bf16[16,20,8,256]{3,2,1,0:T(8,128)(2,1)S(1)}, bf16[16,20,8,256]{3,2,1,0:T(8,128)(2,1)}, u32[]{:S(2)}) copy-start(bf16[16,20,8,256]{3,2,1,0:T(8,128)(2,1)} %get-tuple-element.25) | copy-start | bytes 3932164
  59.4 1.4 %collective-permute-start.1 = (bf16[256,256]{1,0:T(8,128)(2,1)S(1)}, bf16[256,256]{1,0:T(8,128)(2,1)S(1)}, u32[]{:S(2)}, u32[]{:S(2)}) collective-permute-start(bf16[256,256]{1,0:T(8,128)(2,1)S(1)} %row_grad.1.g_ref), channel_id=1, source_target_pairs={{0,16},{16,0},{1,17},{17,1},{2,18},{18,2},{3,19},{19,3},{4,20},{20... | collective-permute-start | bytes 393224 | tf_op jit(solution)/shard_map/ppermute | solution.py:371

commit v4 on v3

--- a/solution.py
+++ b/solution.py
@@ -141,7 +141,7 @@
 def attention_kernel(
     q_ref, do_ref, ckv_ref, nkv_ref, mask_ref,
     out_ref, dq_ref, dkv_ref, dnkv_ref,
-    kx_ref, vx_ref, qx_ref, dox_ref, e_ref, p_ref, ds_ref,
+    kx_ref, vx_ref, qx_ref, dox_ref, p_ref, ds_ref,
 ):
     hd = 128
     tok, heads = q_ref.shape[0], q_ref.shape[1] // hd
@@ -172,7 +172,6 @@
         at = pl.ds(pl.multiple_of(g * group, group), group)
         s = transposed(qx_ref[at, :], kx_ref[...])
         e = jnp.exp2((s - jnp.max(s, axis=1, keepdims=True)) * (scale * LOG2E))
-        e_ref[at, :] = e
         p_ref[at, :] = e.astype(BF16)
         return carry
 
@@ -195,7 +194,7 @@
     def slope(g, carry):
         at = pl.ds(pl.multiple_of(g * group, group), group)
         dp = transposed(dox_ref[at, :], vx_ref[...])
-        ds_ref[at, :] = (e_ref[at, :] * dp).astype(BF16)
+        ds_ref[at, :] = (p_ref[at, :].astype(F32) * dp).astype(BF16)
         return carry
 
     lax.fori_loop(0, heads * tok // group, slope, 0, unroll=True)
@@ -246,6 +245,10 @@
 
 def whole(*shape):
     return pl.BlockSpec(shape, lambda *_: (0,) * len(shape))
+
+
+def left(array):
+    return pltpu.with_memory_space_constraint(array, pltpu.HBM)
 
 
 def limit(mib):
@@ -323,7 +326,7 @@
             pltpu.VMEM((rows, 2 * hd), F32),
             pltpu.VMEM((2, 2, width // 2, 128), F32),
         ],
-        compiler_params=limit(63),
+        compiler_params=limit(60),
         cost_estimate=pl.CostEstimate(
             flops=4 * rows * width * hd, bytes_accessed=12 * MIB, transcendentals=0
         ),
@@ -347,18 +350,19 @@
             pltpu.VMEM((total, 2 * hd), BF16),
             pltpu.VMEM((heads * rows, 2 * hd), BF16),
             pltpu.VMEM((heads * rows, 2 * hd), BF16),
-            pltpu.VMEM((heads * rows, total), F32),
             pltpu.VMEM((heads * rows, total), BF16),
             pltpu.VMEM((heads * rows, total), BF16),
         ],
-        compiler_params=limit(60),
+        compiler_params=limit(36),
         cost_estimate=pl.CostEstimate(
             flops=12 * heads * rows * total * hd,
             bytes_accessed=4 * MIB,
             transcendentals=heads * rows * total,
         ),
         name="attend",
-    )(noisy_query[0], out_grad[0], gathered, nkv, mask)
+    )(
+        left(noisy_query[0]), left(out_grad[0]), gathered, left(nkv), left(mask)
+    )
 
     received = lax.all_to_all(dkv, cp, 0, 0, tiled=True)
 

time: 104 us -> 102 us (0.981)
  Pallas kernels: 28 us -> 26.8 us
    pallas_call x1, Pallas kernels: 9.53 us -> 8.29 us  [per_device(): pl.pallas_call(attention_kernel, out_shape=[shape((rows, heads * hd), BF1...]
  transfers between devices with their start and end apart: 3 -> 3, of which waited for: 2 -> 2; matrix products, arithmetic and copies ran while one was open for 0% -> 0% of each run, Pallas kernels for 21% -> 20%
where the time goes in v4:
time: 102 us
  blocking collectives  60.3 us (59%)
  Pallas kernels  26.8 us (26%)
  starting transfers between devices  7.58 us (7%)
  waiting for transfers between devices  5.32 us (5%)
    all_to_all x1, blocking collectives, per_device(): lax.all_to_all(both.reshape(peers, per, zs, 2 * hd), cp, 0, 0, tiled=True)  23.2 us
    all_to_all x1, blocking collectives, per_device(): received = lax.all_to_all(dkv, cp, 0, 0, tiled=True)  20.1 us
    all_to_all x1, blocking collectives, per_device(): term = lax.all_to_all(jnp.swapaxes(term, 0, 1), 'z', 0, 0, tiled=True)  17 us
    pallas_call x1, Pallas kernels, per_device(): pl.pallas_call(prepare_kernel, grid=(zs,), in_specs=[smem] * 5 + [pl.Bloc...  11.8 us
    pallas_call x1, Pallas kernels, per_device(): pl.pallas_call(attention_kernel, out_shape=[shape((rows, heads * hd), BF1...  8.29 us
    all_to_all x1, starting transfers between devices, per_device(): gathered = lax.all_to_all(spread, cp, 0, 0, tiled=True)  7.49 us
    pallas_call x1, Pallas kernels, per_device(): pl.pallas_call(clean_kernel, in_specs=[anywhere, anywhere, pl.BlockSpec(m...  4.92 us
    all_to_all x1, waiting for transfers between devices, per_device(): gathered = lax.all_to_all(spread, cp, 0, 0, tiled=True)  3.99 us
  transfers between devices with their start and end apart: 3, of which 2 were waited for; matrix products, arithmetic and copies ran while one was open for 0% of the time, Pallas kernels for 20%

profile of v4, /device:TPU:2, one launch (start us, length us, event | category | flops | bytes accessed | tf_op | source)
XLA Modules:
  0.0 101.6 jit_solution(12791743830700015845)
XLA Ops:
  0.6 4.9 %clean.1 = (bf16[16,128,256]{2,1,0:T(8,128)(2,1)}, f32[128,128]{1,0:T(8,128)}) custom-call(bf16[128,5120]{1,0:T(8,128)(2,1)} %bitcast.19, bf16[5120,256]{1,0:T(8,128)(2,1)} %w_ref.3, f32[1,128]{1,0:T(1,128)} %bitcast.16), custom_call_target="tpu_custom_call" | custom-call | flops 335544320 | bytes 5242880 | tf_op jit(solution)/shard_map/clean/pallas_call | solution.py:279
  5.6 7.5 %all-to-all-start = ((bf16[16,128,256]{2,1,0:T(8,128)(2,1)}), bf16[16,128,256]{2,1,0:T(8,128)(2,1)S(1)}, u32[]{:S(2)}, u32[]{:S(2)}) async-start(bf16[16,128,256]{2,1,0:T(8,128)(2,1)} %get-tuple-element.18), calls=%async_computation | async-start | bytes 2097152 | tf_op jit(solution)/shard_map/all_to_all | solution.py:300
  13.0 11.8 %prepare.1 = (bf16[128,256]{1,0:T(8,128)(2,1)}, f32[128,128]{1,0:T(8,128)}, bf16[2176,128]{1,0:T(8,128)(2,1)}, bf16[16,20,8,256]{3,2,1,0:T(8,128)(2,1)}, bf16[16,20,8,256]{3,2,1,0:T(8,128)(2,1)}) custom-call(s32[1,1]{1,0:T(1,128)} %bitcast.5.cp_ref, s32[1,1]{1,0:T(1,128)} %bitcast.6.core_ref, s32[1,4]{1,0:T(1,128)} %len_ref.1, s32[1,32]{1,0:T(1,128)} %cplace_ref.1, ...), custom_call_target="tpu_custom_call" | custom-call | flops 335544320 | bytes 12582912 | tf_op jit(solution)/shard_map/prepare/pallas_call | solution.py:305
  24.8 0.0 collective-permute-start
  24.8 4.0 %all-to-all-done.ckv_ref = bf16[16,128,256]{2,1,0:T(8,128)(2,1)S(1)} async-done(((bf16[16,128,256]{2,1,0:T(8,128)(2,1)}), bf16[16,128,256]{2,1,0:T(8,128)(2,1)S(1)}, u32[]{:S(2)}, u32[]{:S(2)}) %all-to-all-start) | async-done | bytes 1048608 | tf_op jit(solution)/shard_map/all_to_all | solution.py:300
  28.8 8.3 %attend.1 = (bf16[128,1024]{1,0:T(8,128)(2,1)}, bf16[128,1024]{1,0:T(8,128)(2,1)}, bf16[16,256,128]{2,1,0:T(8,128)(2,1)S(1)}, f32[256,128]{1,0:T(8,128)S(1)}) custom-call(bf16[128,1024]{1,0:T(8,128)(2,1)} %bitcast.23, bf16[128,1024]{1,0:T(8,128)(2,1)} %bitcast.24, bf16[16,128,256]{2,1,0:T(8,128)(2,1)S(1)} %all-to-all-done.ckv_ref, ...), custom_call_target="tpu_custom_call" | custom-call | flops 3422552064 | bytes 4194304 | tf_op jit(solution)/shard_map/attend/pallas_call | solution.py:340
  37.1 0.0 copy-start.1
  37.2 0.0 copy-start.2
  37.2 0.0 copy-start.3
  37.2 0.0 copy-start
  37.2 20.1 %all_to_all.20.recv_ref = bf16[16,256,128]{2,1,0:T(8,128)(2,1)S(1)} all-to-all(bf16[16,256,128]{2,1,0:T(8,128)(2,1)S(1)} %get-tuple-element.27), channel_id=1, replica_groups=mesh['z'=8,'core'=2,'y'=4,'x'=4] {'y','x'}, dimensions={0} | all-to-all | bytes 2097152 | tf_op jit(solution)/shard_map/all_to_all | solution.py:367
  57.3 0.0 copy-done.1
  57.3 0.0 copy-done.2
  57.3 0.0 copy-done.3
  57.3 0.4 row_grad.1.g_ref
  57.7 0.1 collective-permute-start.1
  57.8 0.0 collective-permute-done
  57.8 1.3 %collective-permute-done.1.their_g_ref = bf16[256,256]{1,0:T(8,128)(2,1)S(1)} collective-permute-done((bf16[256,256]{1,0:T(8,128)(2,1)S(1)}, bf16[256,256]{1,0:T(8,128)(2,1)S(1)}, u32[]{:S(2)}, u32[]{:S(2)}) %collective-permute-start.1) | collective-permute-done | bytes 131104 | tf_op jit(solution)/shard_map/ppermute | solution.py:375
  59.2 0.0 copy-done
  59.2 1.3 %weight.1 = bf16[2560,256]{1,0:T(8,128)(2,1)S(1)} custom-call(bf16[2560,256]{1,0:T(8,128)(2,1)S(1)} %bitcast.14, bf16[2560,256]{1,0:T(8,128)(2,1)S(1)} %bitcast.15, bf16[256,256]{1,0:T(8,128)(2,1)S(1)} %row_grad.1.g_ref, bf16[256,256]{1,0:T(8,128)(2,1)S(1)} %collective-permute-done.1.their_g_ref), custom_call_target="tpu_custom_call" | custom-call | tf_op jit(solution)/shard_map/weight/pallas_call | solution.py:380
  60.5 23.2 %all_to_all.21 = bf16[16,20,8,256]{3,2,1,0:T(8,128)(2,1)S(1)} all-to-all(bf16[16,20,8,256]{3,2,1,0:T(8,128)(2,1)S(1)} %bitcast.13), channel_id=1, replica_groups=mesh['z'=8,'core'=2,'y'=4,'x'=4] {'y','x'}, dimensions={0} | all-to-all | bytes 2621440 | tf_op jit(solution)/shard_map/all_to_all | solution.py:391
  83.7 0.2 reduce_sum.24
  84.0 17.0 %all_to_all.22 = bf16[8,20,256]{2,1,0:T(8,128)(2,1)S(1)} all-to-all(bf16[8,20,256]{2,1,0:T(8,128)(2,1)S(1)} %copy.12), channel_id=1, replica_groups=mesh['z'=8,'core'=2,'y'=4,'x'=4] {'z'}, dimensions={0} | all-to-all | bytes 163840 | tf_op jit(solution)/shard_map/all_to_all | solution.py:393
  100.9 0.6 reduce_sum.25
  (1 shorter events, 0.0 us)
Async XLA Ops:
  5.6 23.3 %all-to-all-start = ((bf16[16,128,256]{2,1,0:T(8,128)(2,1)}), bf16[16,128,256]{2,1,0:T(8,128)(2,1)S(1)}, u32[]{:S(2)}, u32[]{:S(2)}) async-start(bf16[16,128,256]{2,1,0:T(8,128)(2,1)} %get-tuple-element.18), calls=%async_computation | async-start | bytes 2097152 | tf_op jit(solution)/shard_map/all_to_all | solution.py:300
  24.8 33.0 %collective-permute-start = (bf16[16,20,8,256]{3,2,1,0:T(8,128)(2,1)}, bf16[16,20,8,256]{3,2,1,0:T(8,128)(2,1)S(1)}, u32[]{:S(2)}, u32[]{:S(2)}) collective-permute-start(bf16[16,20,8,256]{3,2,1,0:T(8,128)(2,1)} %get-tuple-element.26), channel_id=1, source_target_pairs={{0,16},{16,0},{1,17},{17,1},{2,18},{18,2},{3,19},{19,3},{4,20},{20... | collective-permute-start | bytes 3932168 | tf_op jit(solution)/shard_map/ppermute | solution.py:338
  37.1 20.2 %copy-start.1 = (f32[128,128]{1,0:T(8,128)S(1)}, f32[128,128]{1,0:T(8,128)}, u32[]{:S(2)}) copy-start(f32[128,128]{1,0:T(8,128)} %get-tuple-element.29.cpre_ref) | copy-start | bytes 196612
  37.2 20.2 %copy-start.2 = (f32[128,128]{1,0:T(8,128)S(1)}, f32[128,128]{1,0:T(8,128)}, u32[]{:S(2)}) copy-start(f32[128,128]{1,0:T(8,128)} %get-tuple-element.30.npre_ref) | copy-start | bytes 196612
  37.2 20.1 %copy-start.3 = (f32[128]{0:T(128)S(1)}, f32[128]{0:T(128)}, u32[]{:S(2)}) copy-start(f32[128]{0:T(128)} %param.14) | copy-start | bytes 1540
  37.2 22.0 %copy-start = (bf16[16,20,8,256]{3,2,1,0:T(8,128)(2,1)S(1)}, bf16[16,20,8,256]{3,2,1,0:T(8,128)(2,1)}, u32[]{:S(2)}) copy-start(bf16[16,20,8,256]{3,2,1,0:T(8,128)(2,1)} %get-tuple-element.25) | copy-start | bytes 3932164
  57.7 1.4 %collective-permute-start.1 = (bf16[256,256]{1,0:T(8,128)(2,1)S(1)}, bf16[256,256]{1,0:T(8,128)(2,1)S(1)}, u32[]{:S(2)}, u32[]{:S(2)}) collective-permute-start(bf16[256,256]{1,0:T(8,128)(2,1)S(1)} %row_grad.1.g_ref), channel_id=1, source_target_pairs={{0,16},{16,0},{1,17},{17,1},{2,18},{18,2},{3,19},{19,3},{4,20},{20... | collective-permute-start | bytes 393224 | tf_op jit(solution)/shard_map/ppermute | solution.py:375

commit v5 on v4

--- a/solution.py
+++ b/solution.py
@@ -141,19 +141,20 @@
 def attention_kernel(
     q_ref, do_ref, ckv_ref, nkv_ref, mask_ref,
     out_ref, dq_ref, dkv_ref, dnkv_ref,
-    kx_ref, vx_ref, qx_ref, dox_ref, p_ref, ds_ref,
+    kx_ref, vx_ref, qx_ref, dox_ref, p_ref, ds_ref, mask_sem,
 ):
     hd = 128
     tok, heads = q_ref.shape[0], q_ref.shape[1] // hd
     scale = hd ** (-0.5)
     peers = ckv_ref.shape[0]
     total = kx_ref.shape[0]
+    mask_load = pltpu.make_async_copy(mask_ref, kx_ref.at[:, pl.ds(hd, hd)], mask_sem)
+    mask_load.start()
     for c in range(peers):
         kx_ref[c * tok : (c + 1) * tok, :hd] = ckv_ref[c, :, :hd]
         vx_ref[c * tok : (c + 1) * tok, :hd] = ckv_ref[c, :, hd:]
     kx_ref[peers * tok :, :hd] = nkv_ref[:, :hd]
     vx_ref[peers * tok :, :hd] = nkv_ref[:, hd:]
-    kx_ref[:, hd:] = mask_ref[...]
     vx_ref[:, hd:] = jnp.ones((total, hd), BF16)
     lane = lax.broadcasted_iota(jnp.int32, (tok, hd), 1)
     block = lax.broadcasted_iota(jnp.int32, (tok, hd), 0) // BLK
@@ -162,6 +163,7 @@
         at = slice(h * tok, (h + 1) * tok)
         qx_ref[at, :hd] = q_ref[:, h * hd : (h + 1) * hd]
         qx_ref[at, hd:] = pick
+    mask_load.wait()
 
     def transposed(a, b):
         return lax.dot_general(a, b, (((1,), (1,)), ((), ())), preferred_element_type=F32)
@@ -276,6 +278,7 @@
     parts = 5
     part = width // parts
     anywhere = pl.BlockSpec(memory_space=pl.ANY)
+    vmem = pl.BlockSpec(memory_space=pltpu.VMEM)
     spread, clean_pre = pl.pallas_call(
         clean_kernel,
         in_specs=[anywhere, anywhere, pl.BlockSpec(memory_space=pltpu.VMEM)],
@@ -339,6 +342,7 @@
 
     attention, query_grad, dkv, dnkv = pl.pallas_call(
         attention_kernel,
+        in_specs=[vmem] * 4 + [anywhere],
         out_shape=[
             shape((rows, heads * hd), BF16),
             shape((rows, heads * hd), BF16),
@@ -352,6 +356,7 @@
             pltpu.VMEM((heads * rows, 2 * hd), BF16),
             pltpu.VMEM((heads * rows, total), BF16),
             pltpu.VMEM((heads * rows, total), BF16),
+            pltpu.SemaphoreType.DMA,
         ],
         compiler_params=limit(36),
         cost_estimate=pl.CostEstimate(

time: 102 us -> 103 us (level)
  transfers between devices with their start and end apart: 3 -> 3, of which waited for: 2 -> 2; matrix products, arithmetic and copies ran while one was open for 0% -> 0% of each run, Pallas kernels for 20% -> 21%
where the time goes in v5:
time: 103 us; the launch traced here: 102 us
  blocking collectives  60.3 us (59%)
  Pallas kernels  27.4 us (27%)
  starting transfers between devices  7.58 us (7%)
  waiting for transfers between devices  5.32 us (5%)
    all_to_all x1, blocking collectives, per_device(): lax.all_to_all(both.reshape(peers, per, zs, 2 * hd), cp, 0, 0, tiled=True)  23.2 us
    all_to_all x1, blocking collectives, per_device(): received = lax.all_to_all(dkv, cp, 0, 0, tiled=True)  20.1 us
    all_to_all x1, blocking collectives, per_device(): term = lax.all_to_all(jnp.swapaxes(term, 0, 1), 'z', 0, 0, tiled=True)  17 us
    pallas_call x1, Pallas kernels, per_device(): pl.pallas_call(prepare_kernel, grid=(zs,), in_specs=[smem] * 5 + [pl.Bloc...  11.8 us
    pallas_call x1, Pallas kernels, per_device(): pl.pallas_call(attention_kernel, in_specs=[vmem] * 4 + [anywhere], out_sh...  8.89 us
    all_to_all x1, starting transfers between devices, per_device(): gathered = lax.all_to_all(spread, cp, 0, 0, tiled=True)  7.49 us
    pallas_call x1, Pallas kernels, per_device(): pl.pallas_call(clean_kernel, in_specs=[anywhere, anywhere, pl.BlockSpec(m...  4.92 us
    all_to_all x1, waiting for transfers between devices, per_device(): gathered = lax.all_to_all(spread, cp, 0, 0, tiled=True)  3.99 us
  transfers between devices with their start and end apart: 3, of which 2 were waited for; matrix products, arithmetic and copies ran while one was open for 0% of the time, Pallas kernels for 21%

profile of v5, /device:TPU:2, one launch (start us, length us, event | category | flops | bytes accessed | tf_op | source)
XLA Modules:
  0.0 102.2 jit_solution(15088763556410666135)
XLA Ops:
  0.6 4.9 %clean.1 = (bf16[16,128,256]{2,1,0:T(8,128)(2,1)}, f32[128,128]{1,0:T(8,128)}) custom-call(bf16[128,5120]{1,0:T(8,128)(2,1)} %bitcast.19, bf16[5120,256]{1,0:T(8,128)(2,1)} %w_ref.3, f32[1,128]{1,0:T(1,128)} %bitcast.16), custom_call_target="tpu_custom_call" | custom-call | flops 335544320 | bytes 5242880 | tf_op jit(solution)/shard_map/clean/pallas_call | solution.py:282
  5.6 7.5 %all-to-all-start = ((bf16[16,128,256]{2,1,0:T(8,128)(2,1)}), bf16[16,128,256]{2,1,0:T(8,128)(2,1)S(1)}, u32[]{:S(2)}, u32[]{:S(2)}) async-start(bf16[16,128,256]{2,1,0:T(8,128)(2,1)} %get-tuple-element.18), calls=%async_computation | async-start | bytes 2097152 | tf_op jit(solution)/shard_map/all_to_all | solution.py:303
  13.0 11.8 %prepare.1 = (bf16[128,256]{1,0:T(8,128)(2,1)}, f32[128,128]{1,0:T(8,128)}, bf16[2176,128]{1,0:T(8,128)(2,1)}, bf16[16,20,8,256]{3,2,1,0:T(8,128)(2,1)}, bf16[16,20,8,256]{3,2,1,0:T(8,128)(2,1)}) custom-call(s32[1,1]{1,0:T(1,128)} %bitcast.5.cp_ref, s32[1,1]{1,0:T(1,128)} %bitcast.6.core_ref, s32[1,4]{1,0:T(1,128)} %len_ref.1, s32[1,32]{1,0:T(1,128)} %cplace_ref.1, ...), custom_call_target="tpu_custom_call" | custom-call | flops 335544320 | bytes 12582912 | tf_op jit(solution)/shard_map/prepare/pallas_call | solution.py:308
  24.8 0.0 collective-permute-start
  24.8 4.0 %all-to-all-done.ckv_ref = bf16[16,128,256]{2,1,0:T(8,128)(2,1)S(1)} async-done(((bf16[16,128,256]{2,1,0:T(8,128)(2,1)}), bf16[16,128,256]{2,1,0:T(8,128)(2,1)S(1)}, u32[]{:S(2)}, u32[]{:S(2)}) %all-to-all-start) | async-done | bytes 1048608 | tf_op jit(solution)/shard_map/all_to_all | solution.py:303
  28.8 8.9 %attend.1 = (bf16[128,1024]{1,0:T(8,128)(2,1)}, bf16[128,1024]{1,0:T(8,128)(2,1)}, bf16[16,256,128]{2,1,0:T(8,128)(2,1)S(1)}, f32[256,128]{1,0:T(8,128)S(1)}) custom-call(bf16[128,1024]{1,0:T(8,128)(2,1)} %bitcast.23, bf16[128,1024]{1,0:T(8,128)(2,1)} %bitcast.24, bf16[16,128,256]{2,1,0:T(8,128)(2,1)S(1)} %all-to-all-done.ckv_ref, ...), custom_call_target="tpu_custom_call" | custom-call | flops 3422552064 | bytes 4194304 | tf_op jit(solution)/shard_map/attend/pallas_call | solution.py:343
  37.7 0.0 copy-start.1
  37.8 0.0 copy-start.2
  37.8 0.0 copy-start.3
  37.8 0.0 copy-start
  37.8 20.1 %all_to_all.20.recv_ref = bf16[16,256,128]{2,1,0:T(8,128)(2,1)S(1)} all-to-all(bf16[16,256,128]{2,1,0:T(8,128)(2,1)S(1)} %get-tuple-element.27), channel_id=1, replica_groups=mesh['z'=8,'core'=2,'y'=4,'x'=4] {'y','x'}, dimensions={0} | all-to-all | bytes 2097152 | tf_op jit(solution)/shard_map/all_to_all | solution.py:372
  57.9 0.0 copy-done.1
  57.9 0.0 copy-done.2
  57.9 0.0 copy-done.3
  57.9 0.4 row_grad.1.g_ref
  58.3 0.1 collective-permute-start.1
  58.4 0.0 collective-permute-done
  58.4 1.3 %collective-permute-done.1.their_g_ref = bf16[256,256]{1,0:T(8,128)(2,1)S(1)} collective-permute-done((bf16[256,256]{1,0:T(8,128)(2,1)S(1)}, bf16[256,256]{1,0:T(8,128)(2,1)S(1)}, u32[]{:S(2)}, u32[]{:S(2)}) %collective-permute-start.1) | collective-permute-done | bytes 131104 | tf_op jit(solution)/shard_map/ppermute | solution.py:380
  59.8 0.0 copy-done
  59.8 1.3 %weight.1 = bf16[2560,256]{1,0:T(8,128)(2,1)S(1)} custom-call(bf16[2560,256]{1,0:T(8,128)(2,1)S(1)} %bitcast.14, bf16[2560,256]{1,0:T(8,128)(2,1)S(1)} %bitcast.15, bf16[256,256]{1,0:T(8,128)(2,1)S(1)} %row_grad.1.g_ref, bf16[256,256]{1,0:T(8,128)(2,1)S(1)} %collective-permute-done.1.their_g_ref), custom_call_target="tpu_custom_call" | custom-call | tf_op jit(solution)/shard_map/weight/pallas_call | solution.py:385
  61.1 23.2 %all_to_all.21 = bf16[16,20,8,256]{3,2,1,0:T(8,128)(2,1)S(1)} all-to-all(bf16[16,20,8,256]{3,2,1,0:T(8,128)(2,1)S(1)} %bitcast.13), channel_id=1, replica_groups=mesh['z'=8,'core'=2,'y'=4,'x'=4] {'y','x'}, dimensions={0} | all-to-all | bytes 2621440 | tf_op jit(solution)/shard_map/all_to_all | solution.py:396
  84.4 0.2 reduce_sum.24
  84.6 17.0 %all_to_all.22 = bf16[8,20,256]{2,1,0:T(8,128)(2,1)S(1)} all-to-all(bf16[8,20,256]{2,1,0:T(8,128)(2,1)S(1)} %copy.12), channel_id=1, replica_groups=mesh['z'=8,'core'=2,'y'=4,'x'=4] {'z'}, dimensions={0} | all-to-all | bytes 163840 | tf_op jit(solution)/shard_map/all_to_all | solution.py:398
  101.6 0.6 reduce_sum.25
  (1 shorter events, 0.0 us)
Async XLA Ops:
  5.6 23.3 %all-to-all-start = ((bf16[16,128,256]{2,1,0:T(8,128)(2,1)}), bf16[16,128,256]{2,1,0:T(8,128)(2,1)S(1)}, u32[]{:S(2)}, u32[]{:S(2)}) async-start(bf16[16,128,256]{2,1,0:T(8,128)(2,1)} %get-tuple-element.18), calls=%async_computation | async-start | bytes 2097152 | tf_op jit(solution)/shard_map/all_to_all | solution.py:303
  24.8 33.6 %collective-permute-start = (bf16[16,20,8,256]{3,2,1,0:T(8,128)(2,1)}, bf16[16,20,8,256]{3,2,1,0:T(8,128)(2,1)S(1)}, u32[]{:S(2)}, u32[]{:S(2)}) collective-permute-start(bf16[16,20,8,256]{3,2,1,0:T(8,128)(2,1)} %get-tuple-element.26), channel_id=1, source_target_pairs={{0,16},{16,0},{1,17},{17,1},{2,18},{18,2},{3,19},{19,3},{4,20},{20... | collective-permute-start | bytes 3932168 | tf_op jit(solution)/shard_map/ppermute | solution.py:341
  37.7 20.2 %copy-start.1 = (f32[128,128]{1,0:T(8,128)S(1)}, f32[128,128]{1,0:T(8,128)}, u32[]{:S(2)}) copy-start(f32[128,128]{1,0:T(8,128)} %get-tuple-element.29.cpre_ref) | copy-start | bytes 196612
  37.8 20.2 %copy-start.2 = (f32[128,128]{1,0:T(8,128)S(1)}, f32[128,128]{1,0:T(8,128)}, u32[]{:S(2)}) copy-start(f32[128,128]{1,0:T(8,128)} %get-tuple-element.30.npre_ref) | copy-start | bytes 196612
  37.8 20.2 %copy-start.3 = (f32[128]{0:T(128)S(1)}, f32[128]{0:T(128)}, u32[]{:S(2)}) copy-start(f32[128]{0:T(128)} %param.14) | copy-start | bytes 1540
  37.8 22.0 %copy-start = (bf16[16,20,8,256]{3,2,1,0:T(8,128)(2,1)S(1)}, bf16[16,20,8,256]{3,2,1,0:T(8,128)(2,1)}, u32[]{:S(2)}) copy-start(bf16[16,20,8,256]{3,2,1,0:T(8,128)(2,1)} %get-tuple-element.25) | copy-start | bytes 3932164
  58.3 1.4 %collective-permute-start.1 = (bf16[256,256]{1,0:T(8,128)(2,1)S(1)}, bf16[256,256]{1,0:T(8,128)(2,1)S(1)}, u32[]{:S(2)}, u32[]{:S(2)}) collective-permute-start(bf16[256,256]{1,0:T(8,128)(2,1)S(1)} %row_grad.1.g_ref), channel_id=1, source_target_pairs={{0,16},{16,0},{1,17},{17,1},{2,18},{18,2},{3,19},{19,3},{4,20},{20... | collective-permute-start | bytes 393224 | tf_op jit(solution)/shard_map/ppermute | solution.py:380
